TPU v7x, 256 devices: a whole 4x4x8 slice. The times are simulated.
256 devices in a mesh: group: 4 (over y_lo, core), ctx: 64 (over x, z, y_hi).
Axes of the slice: x: 4, y: 4 (y_hi: 2, y_lo: 2; y = y_hi * 2 + y_lo), z: 8, core: 2. Of those that a mesh axis runs over, the one named last changes fastest.
Arguments:
- hidden: bfloat16 [4, 8192, 5120], P('group', 'ctx'), may hold values from -6 to 6
- queries: bfloat16 [4, 8192, 2560], P('group', 'ctx'), may hold values from -300 to 300
- key_value_weight: bfloat16 [5120, 1024], P(('group', 'ctx')), may hold values from -0.078125 to 0.078125
- pooled_hidden_states: bfloat16 [64, 16, 5120], P('ctx'), may hold values from -6 to 6
- group_page_table: int32 [4, 32], P('group'), may hold values from 0 to 63, as said below
- resp_lengths: int32 [4, 8], P('group'), may hold values from 1 to 2048, 8192 in all within a row
Outputs:
- attended: bfloat16 [4, 8192, 2560], P('group', 'ctx')
Inputs may be any that keep to these rules, and one draw needn't show every extreme that they name: `group_page_table`: each row names 32 different pages of the pool. `resp_lengths`: each row sums to 8192.
All inputs are finite; a program needn't handle non-finite values.
Results may differ from a plain program's by a relative error of at most 0.012.
The roundings to bfloat16 on the way count: a program that leaves them out, or rounds other values in their place, can miss the bound.
Values may be sent and summed in bfloat16 or wider, within the bound.
A program may use at most 128 MiB of HBM per device.

v0:
```python
import math

import jax
import jax.numpy as jnp
from jax import lax
from jax.sharding import PartitionSpec as P

QUERY_HEADS = 20
KEY_VALUE_HEADS = 4
HEAD_SIZE = 128
DEVICE_TOKENS = 128
PAGE_TOKENS = 16


def passed_along(block, axis, distance):
    devices = range(lax.axis_size(axis))
    route = [(i - distance, i) for i in devices if i - distance in devices]
    return lax.ppermute(block, axis, route)


def apply_projection(rows, weight):
    return jnp.dot(rows, weight, preferred_element_type=jnp.float32).astype(jnp.bfloat16)


def response_ids(lengths, positions):
    ends = jnp.cumsum(lengths)
    return jnp.sum((positions[:, None] >= ends[None, :]).astype(jnp.int32), axis=1)


def absorb(state, query_matrix, key_rows, value_rows, live, scale):
    top, total, accum = state
    scores = (
        jnp.einsum("qgrd,kgd->grqk", query_matrix, key_rows, preferred_element_type=jnp.float32)
        * scale
    )
    scores = jnp.where(live[None, None], scores, -jnp.inf)
    new_top = jnp.maximum(top, jnp.max(scores, axis=3))
    factor = jnp.exp(top - new_top)
    weights = jnp.exp(scores - new_top[..., None])
    total = total * factor + jnp.sum(weights, axis=3)
    accum = accum * factor[..., None] + jnp.einsum(
        "grqk,kgd->grqd",
        weights.astype(jnp.bfloat16),
        value_rows,
        preferred_element_type=jnp.float32,
    )
    return (new_top, total, accum)


def body(hidden, queries, key_value_weight, pooled_hidden_states, group_page_table, resp_lengths):
    column_width = KEY_VALUE_HEADS * HEAD_SIZE
    scale = 1.0 / math.sqrt(HEAD_SIZE)
    full_weight = lax.all_gather(key_value_weight, ("group", "ctx"), axis=0, tiled=True)
    own_kv = apply_projection(hidden[0], full_weight)
    pooled_key_value = apply_projection(
        pooled_hidden_states.reshape(-1, pooled_hidden_states.shape[2]), full_weight
    )
    pool_all = lax.all_gather(pooled_key_value, "ctx", axis=0, tiled=True).reshape(
        -1, PAGE_TOKENS, 2 * column_width
    )
    prompt_key_value = jnp.take(pool_all, group_page_table[0], axis=0).reshape(-1, 2 * column_width)
    lengths = resp_lengths[0]
    query_matrix = queries[0].reshape(
        DEVICE_TOKENS, KEY_VALUE_HEADS, QUERY_HEADS // KEY_VALUE_HEADS, HEAD_SIZE
    )
    first = lax.axis_index("ctx") * DEVICE_TOKENS
    q_pos = first + jnp.arange(DEVICE_TOKENS, dtype=jnp.int32)
    q_ids = response_ids(lengths, q_pos)
    dimension_list = (KEY_VALUE_HEADS, QUERY_HEADS // KEY_VALUE_HEADS, DEVICE_TOKENS)
    state = (
        jnp.full(dimension_list, -jnp.inf, jnp.float32),
        jnp.zeros(dimension_list, jnp.float32),
        jnp.zeros(dimension_list + (HEAD_SIZE,), jnp.float32),
    )
    prompt_token_rows = prompt_key_value.shape[0]
    prompt_live = jnp.ones((DEVICE_TOKENS, prompt_token_rows), dtype=bool)
    state = absorb(
        state,
        query_matrix,
        prompt_key_value[:, :column_width].reshape(prompt_token_rows, KEY_VALUE_HEADS, HEAD_SIZE),
        prompt_key_value[:, column_width:].reshape(prompt_token_rows, KEY_VALUE_HEADS, HEAD_SIZE),
        prompt_live,
        scale,
    )

    def block_step(carry, key_value_rows, k_first):
        count_of_rows = key_value_rows.shape[0]
        k_pos = k_first + jnp.arange(count_of_rows, dtype=jnp.int32)
        k_ids = response_ids(lengths, k_pos)
        live = (
            (k_pos[None, :] <= q_pos[:, None])
            & (k_pos[None, :] >= 0)
            & (k_ids[None, :] == q_ids[:, None])
        )
        key_rows = key_value_rows[:, :column_width].reshape(
            count_of_rows, KEY_VALUE_HEADS, HEAD_SIZE
        )
        value_rows = key_value_rows[:, column_width:].reshape(
            count_of_rows, KEY_VALUE_HEADS, HEAD_SIZE
        )
        return absorb(carry, query_matrix, key_rows, value_rows, live, scale)

    state = block_step(state, own_kv, first)
    reach_steps = lax.axis_size("ctx") // 4

    def near_step(page_index, carry):
        moving, inner_state = carry
        moving = passed_along(moving, "ctx", 1)
        return (moving, block_step(inner_state, moving, first - (page_index + 1) * DEVICE_TOKENS))

    state = lax.fori_loop(0, reach_steps, near_step, (own_kv, state))[1]
    mixed = state[2] / state[1][..., None]
    return (
        jnp.transpose(mixed, (2, 0, 1, 3))
        .reshape(1, DEVICE_TOKENS, QUERY_HEADS * HEAD_SIZE)
        .astype(jnp.bfloat16)
    )


def solution(mesh):
    in_specs = (
        P("group", "ctx", None),
        P("group", "ctx", None),
        P(("group", "ctx"), None),
        P("ctx", None, None),
        P("group", None),
        P("group", None),
    )
    out_specs = P("group", "ctx", None)
    return jax.shard_map(body, mesh=mesh, in_specs=in_specs, out_specs=out_specs, check_vma=False)
```

profile of v0, /device:TPU:14, one launch (start us, length us, event | category | flops | bytes accessed | tf_op | source)
XLA Modules:
  0.0 1159.6 jit_solution(13307806452107943136)
XLA Ops:
  7.3 724.0 %all-gather.6.cloned.1.call-done = bf16[256,20,1024]{2,1,0:T(8,128)(2,1)} async-done(((bf16[1,20,1024]{2,1,0:T(8,128)(2,1)}), bf16[256,20,1024]{2,1,0:T(8,128)(2,1)}) %all-gather.6.cloned.1.call-update) | async-done | bytes 10485776 | tf_op jit(solution)/shard_map/all_gather | solution.py:53
  731.3 16.4 %reshape.326 = bf16[5120,1024]{1,0:T(8,128)(2,1)} reshape(bf16[256,20,1024]{2,1,0:T(8,128)(2,1)} %all-gather.6.cloned.1.call-done) | data formatting | bytes 20971520
  747.7 6.1 convolution_convert_fusion
  757.7 5.5 fusion.25
  766.2 111.3 %all-gather.4.cloned.1.call-done = bf16[1024,1024]{1,0:T(8,128)(2,1)} async-done(((bf16[16,1024]{1,0:T(8,128)(2,1)}), bf16[1024,1024]{1,0:T(8,128)(2,1)}) %all-gather.4.cloned.1.call-update) | async-done | bytes 2097168 | tf_op jit(solution)/shard_map/all_gather | solution.py:58
  892.8 3.7 fusion.20
  897.0 251.8 %while.23 = (s32[]{:T(128)}, bf16[128,1024]{0,1:T(8,128)(2,1)}, f32[4,5,128]{2,1,0:T(8,128)S(1)}, f32[4,5,128]{2,1,0:T(8,128)}, f32[4,5,128,128]{3,2,1,0:T(8,128...) while((s32[]{:T(128)}, bf16[128,1024]{0,1:T(8,128)(2,1)}, ...), condition=%wide.region_11.12_spmd.clone.clone, body=%wide.region_7.11_spmd.clone.clone.sunk | while | flops 170795392 | bytes 9851409 | solution.py:111
  897.0 3.3 collective-permute-start
  901.8 8.2 collective-permute-done
  915.7 9.6 collective-permute-done
  931.0 9.6 collective-permute-done
  946.2 9.6 collective-permute-done
  961.5 9.6 collective-permute-done
  976.8 9.6 collective-permute-done
  992.1 9.7 collective-permute-done
  1007.4 10.7 collective-permute-done
  1023.9 12.0 %collective-permute-done = bf16[128,1024]{0,1:T(8,128)(2,1)S(1)} collective-permute-done((bf16[128,1024]{0,1:T(8,128)(2,1)}, bf16[128,1024]{0,1:T(8,128)(2,1)S(1)}, u32[]{:S(2)}, u32[]{:S(2)}) %collective-permute-start) | collective-permute-done | bytes 262176 | tf_op jit(solution)/shard_map/while/body/eval_jaxpr/ppermute | solution.py:18
  1041.6 11.6 %collective-permute-done = bf16[128,1024]{0,1:T(8,128)(2,1)S(1)} collective-permute-done((bf16[128,1024]{0,1:T(8,128)(2,1)}, bf16[128,1024]{0,1:T(8,128)(2,1)S(1)}, u32[]{:S(2)}, u32[]{:S(2)}) %collective-permute-start) | collective-permute-done | bytes 262176 | tf_op jit(solution)/shard_map/while/body/eval_jaxpr/ppermute | solution.py:18
  1058.9 10.8 collective-permute-done
  1075.4 9.9 collective-permute-done
  1091.0 9.6 collective-permute-done
  1106.3 9.6 collective-permute-done
  1121.6 9.6 collective-permute-done
  1136.9 9.6 collective-permute-done
  (335 shorter events, 115.1 us)
Async XLA Ops:
  6.5 751.1 %copy-start = (bf16[1,128,5120]{2,1,0:T(8,128)(2,1)S(1)}, bf16[1,128,5120]{2,1,0:T(8,128)(2,1)}, u32[]{:S(2)}) copy-start(bf16[1,128,5120]{2,1,0:T(8,128)(2,1)} %param.8) | copy-start | bytes 3932164
  6.5 724.7 %all-gather.6.cloned.1.call-start = ((), (), s32[]{:S(2)}) async-start(), calls=%async_computation.1 | async-start | bytes 12632064 | tf_op jit(solution)/shard_map/all_gather | solution.py:53
  7.3 740.5 %copy-start.10 = (bf16[1,16,5120]{2,1,0:T(8,128)(2,1)S(1)}, bf16[1,16,5120]{2,1,0:T(8,128)(2,1)}, u32[]{:S(2)}) copy-start(bf16[1,16,5120]{2,1,0:T(8,128)(2,1)} %param.11) | copy-start | bytes 491524
  7.3 870.1 %all-gather.4.cloned.1.call-start = ((), (), s32[]{:S(2)}) async-start(), calls=%async_computation | async-start | bytes 2129920 | tf_op jit(solution)/shard_map/all_gather | solution.py:58
  747.7 6.9 copy-start.9
  755.0 8.2 copy-start.4
  766.2 125.6 %copy-start.2 = (f32[4,5,128,128]{2,3,1,0:T(8,128)}, f32[4,5,128,128]{2,3,1,0:T(8,128)S(1)}, u32[]{:S(2)}) copy-start(f32[4,5,128,128]{2,3,1,0:T(8,128)S(1)} %get-tuple-element.358) | copy-start | bytes 3932164
  766.2 114.6 %copy-start.13 = (pred[512]{0:T(512)(128)(4,1)S(1)}, pred[512]{0:T(512)(128)(4,1)}, u32[]{:S(2)}) copy-start(pred[512]{0:T(512)(128)(4,1)} %broadcast_in_dim.116) | copy-start | bytes 1540
  897.0 13.0 %collective-permute-start = (bf16[128,1024]{0,1:T(8,128)(2,1)}, bf16[128,1024]{0,1:T(8,128)(2,1)S(1)}, u32[]{:S(2)}, u32[]{:S(2)}) collective-permute-start(bf16[128,1024]{0,1:T(8,128)(2,1)} %get-tuple-element.442), channel_id=1, source_target_pairs={{0,1},{1,2},{2,3},{3,4},{4,5},{5,6},{6,7},{7,8},{8,9},{9,10},{10,1... | collective-permute-start | bytes 786440 | tf_op jit(solution)/shard_map/while/body/eval_jaxpr/ppermute | solution.py:18
  912.3 13.0 %collective-permute-start = (bf16[128,1024]{0,1:T(8,128)(2,1)}, bf16[128,1024]{0,1:T(8,128)(2,1)S(1)}, u32[]{:S(2)}, u32[]{:S(2)}) collective-permute-start(bf16[128,1024]{0,1:T(8,128)(2,1)} %get-tuple-element.442), channel_id=1, source_target_pairs={{0,1},{1,2},{2,3},{3,4},{4,5},{5,6},{6,7},{7,8},{8,9},{9,10},{10,1... | collective-permute-start | bytes 786440 | tf_op jit(solution)/shard_map/while/body/eval_jaxpr/ppermute | solution.py:18
  927.5 13.0 %collective-permute-start = (bf16[128,1024]{0,1:T(8,128)(2,1)}, bf16[128,1024]{0,1:T(8,128)(2,1)S(1)}, u32[]{:S(2)}, u32[]{:S(2)}) collective-permute-start(bf16[128,1024]{0,1:T(8,128)(2,1)} %get-tuple-element.442), channel_id=1, source_target_pairs={{0,1},{1,2},{2,3},{3,4},{4,5},{5,6},{6,7},{7,8},{8,9},{9,10},{10,1... | collective-permute-start | bytes 786440 | tf_op jit(solution)/shard_map/while/body/eval_jaxpr/ppermute | solution.py:18
  942.8 13.0 %collective-permute-start = (bf16[128,1024]{0,1:T(8,128)(2,1)}, bf16[128,1024]{0,1:T(8,128)(2,1)S(1)}, u32[]{:S(2)}, u32[]{:S(2)}) collective-permute-start(bf16[128,1024]{0,1:T(8,128)(2,1)} %get-tuple-element.442), channel_id=1, source_target_pairs={{0,1},{1,2},{2,3},{3,4},{4,5},{5,6},{6,7},{7,8},{8,9},{9,10},{10,1... | collective-permute-start | bytes 786440 | tf_op jit(solution)/shard_map/while/body/eval_jaxpr/ppermute | solution.py:18
  958.1 13.0 %collective-permute-start = (bf16[128,1024]{0,1:T(8,128)(2,1)}, bf16[128,1024]{0,1:T(8,128)(2,1)S(1)}, u32[]{:S(2)}, u32[]{:S(2)}) collective-permute-start(bf16[128,1024]{0,1:T(8,128)(2,1)} %get-tuple-element.442), channel_id=1, source_target_pairs={{0,1},{1,2},{2,3},{3,4},{4,5},{5,6},{6,7},{7,8},{8,9},{9,10},{10,1... | collective-permute-start | bytes 786440 | tf_op jit(solution)/shard_map/while/body/eval_jaxpr/ppermute | solution.py:18
  973.4 13.0 %collective-permute-start = (bf16[128,1024]{0,1:T(8,128)(2,1)}, bf16[128,1024]{0,1:T(8,128)(2,1)S(1)}, u32[]{:S(2)}, u32[]{:S(2)}) collective-permute-start(bf16[128,1024]{0,1:T(8,128)(2,1)} %get-tuple-element.442), channel_id=1, source_target_pairs={{0,1},{1,2},{2,3},{3,4},{4,5},{5,6},{6,7},{7,8},{8,9},{9,10},{10,1... | collective-permute-start | bytes 786440 | tf_op jit(solution)/shard_map/while/body/eval_jaxpr/ppermute | solution.py:18
  988.6 13.1 %collective-permute-start = (bf16[128,1024]{0,1:T(8,128)(2,1)}, bf16[128,1024]{0,1:T(8,128)(2,1)S(1)}, u32[]{:S(2)}, u32[]{:S(2)}) collective-permute-start(bf16[128,1024]{0,1:T(8,128)(2,1)} %get-tuple-element.442), channel_id=1, source_target_pairs={{0,1},{1,2},{2,3},{3,4},{4,5},{5,6},{6,7},{7,8},{8,9},{9,10},{10,1... | collective-permute-start | bytes 786440 | tf_op jit(solution)/shard_map/while/body/eval_jaxpr/ppermute | solution.py:18
  1004.0 14.2 %collective-permute-start = (bf16[128,1024]{0,1:T(8,128)(2,1)}, bf16[128,1024]{0,1:T(8,128)(2,1)S(1)}, u32[]{:S(2)}, u32[]{:S(2)}) collective-permute-start(bf16[128,1024]{0,1:T(8,128)(2,1)} %get-tuple-element.442), channel_id=1, source_target_pairs={{0,1},{1,2},{2,3},{3,4},{4,5},{5,6},{6,7},{7,8},{8,9},{9,10},{10,1... | collective-permute-start | bytes 786440 | tf_op jit(solution)/shard_map/while/body/eval_jaxpr/ppermute | solution.py:18
  1020.5 15.4 %collective-permute-start = (bf16[128,1024]{0,1:T(8,128)(2,1)}, bf16[128,1024]{0,1:T(8,128)(2,1)S(1)}, u32[]{:S(2)}, u32[]{:S(2)}) collective-permute-start(bf16[128,1024]{0,1:T(8,128)(2,1)} %get-tuple-element.442), channel_id=1, source_target_pairs={{0,1},{1,2},{2,3},{3,4},{4,5},{5,6},{6,7},{7,8},{8,9},{9,10},{10,1... | collective-permute-start | bytes 786440 | tf_op jit(solution)/shard_map/while/body/eval_jaxpr/ppermute | solution.py:18
  1038.2 15.0 %collective-permute-start = (bf16[128,1024]{0,1:T(8,128)(2,1)}, bf16[128,1024]{0,1:T(8,128)(2,1)S(1)}, u32[]{:S(2)}, u32[]{:S(2)}) collective-permute-start(bf16[128,1024]{0,1:T(8,128)(2,1)} %get-tuple-element.442), channel_id=1, source_target_pairs={{0,1},{1,2},{2,3},{3,4},{4,5},{5,6},{6,7},{7,8},{8,9},{9,10},{10,1... | collective-permute-start | bytes 786440 | tf_op jit(solution)/shard_map/while/body/eval_jaxpr/ppermute | solution.py:18
  1055.5 14.2 %collective-permute-start = (bf16[128,1024]{0,1:T(8,128)(2,1)}, bf16[128,1024]{0,1:T(8,128)(2,1)S(1)}, u32[]{:S(2)}, u32[]{:S(2)}) collective-permute-start(bf16[128,1024]{0,1:T(8,128)(2,1)} %get-tuple-element.442), channel_id=1, source_target_pairs={{0,1},{1,2},{2,3},{3,4},{4,5},{5,6},{6,7},{7,8},{8,9},{9,10},{10,1... | collective-permute-start | bytes 786440 | tf_op jit(solution)/shard_map/while/body/eval_jaxpr/ppermute | solution.py:18
  1072.0 13.3 %collective-permute-start = (bf16[128,1024]{0,1:T(8,128)(2,1)}, bf16[128,1024]{0,1:T(8,128)(2,1)S(1)}, u32[]{:S(2)}, u32[]{:S(2)}) collective-permute-start(bf16[128,1024]{0,1:T(8,128)(2,1)} %get-tuple-element.442), channel_id=1, source_target_pairs={{0,1},{1,2},{2,3},{3,4},{4,5},{5,6},{6,7},{7,8},{8,9},{9,10},{10,1... | collective-permute-start | bytes 786440 | tf_op jit(solution)/shard_map/while/body/eval_jaxpr/ppermute | solution.py:18
  1087.6 13.0 %collective-permute-start = (bf16[128,1024]{0,1:T(8,128)(2,1)}, bf16[128,1024]{0,1:T(8,128)(2,1)S(1)}, u32[]{:S(2)}, u32[]{:S(2)}) collective-permute-start(bf16[128,1024]{0,1:T(8,128)(2,1)} %get-tuple-element.442), channel_id=1, source_target_pairs={{0,1},{1,2},{2,3},{3,4},{4,5},{5,6},{6,7},{7,8},{8,9},{9,10},{10,1... | collective-permute-start | bytes 786440 | tf_op jit(solution)/shard_map/while/body/eval_jaxpr/ppermute | solution.py:18
  1102.9 13.0 %collective-permute-start = (bf16[128,1024]{0,1:T(8,128)(2,1)}, bf16[128,1024]{0,1:T(8,128)(2,1)S(1)}, u32[]{:S(2)}, u32[]{:S(2)}) collective-permute-start(bf16[128,1024]{0,1:T(8,128)(2,1)} %get-tuple-element.442), channel_id=1, source_target_pairs={{0,1},{1,2},{2,3},{3,4},{4,5},{5,6},{6,7},{7,8},{8,9},{9,10},{10,1... | collective-permute-start | bytes 786440 | tf_op jit(solution)/shard_map/while/body/eval_jaxpr/ppermute | solution.py:18
  1118.2 13.0 %collective-permute-start = (bf16[128,1024]{0,1:T(8,128)(2,1)}, bf16[128,1024]{0,1:T(8,128)(2,1)S(1)}, u32[]{:S(2)}, u32[]{:S(2)}) collective-permute-start(bf16[128,1024]{0,1:T(8,128)(2,1)} %get-tuple-element.442), channel_id=1, source_target_pairs={{0,1},{1,2},{2,3},{3,4},{4,5},{5,6},{6,7},{7,8},{8,9},{9,10},{10,1... | collective-permute-start | bytes 786440 | tf_op jit(solution)/shard_map/while/body/eval_jaxpr/ppermute | solution.py:18
  1133.4 13.0 %collective-permute-start = (bf16[128,1024]{0,1:T(8,128)(2,1)}, bf16[128,1024]{0,1:T(8,128)(2,1)S(1)}, u32[]{:S(2)}, u32[]{:S(2)}) collective-permute-start(bf16[128,1024]{0,1:T(8,128)(2,1)} %get-tuple-element.442), channel_id=1, source_target_pairs={{0,1},{1,2},{2,3},{3,4},{4,5},{5,6},{6,7},{7,8},{8,9},{9,10},{10,1... | collective-permute-start | bytes 786440 | tf_op jit(solution)/shard_map/while/body/eval_jaxpr/ppermute | solution.py:18
  (40 other events, 43.1 us)
Sparse Core Ops, SparseCore 0:
  9.2 722.0 all-gather.5
  754.0 123.3 all-gather.3
where the time goes:
time: 1160 us
  waiting for transfers between devices  995 us (86%)
  local copies, waits for them, and re-layouts  44.9 us (4%)
  matrix products  39.3 us (3%)
  other arithmetic  33.3 us (3%)
  starting transfers between devices  32 us (3%)
  between operations  13.6 us (1%)
    all_gather x1, waiting for transfers between devices, body(): lax.all_gather(key_value_weight, ('group', 'ctx'), axis=0, tiled=True)  724 us
    ppermute x16, waiting for transfers between devices, passed_along(): return lax.ppermute(block, axis, route)  159 us
    all_gather x1, waiting for transfers between devices, body(): lax.all_gather(pooled_key_value, 'ctx', axis=0, tiled=True)  111 us
    ppermute x16, starting transfers between devices, passed_along(): return lax.ppermute(block, axis, route)  31.9 us
  transfers between devices with their start and end apart: 18, of which 18 were waited for; matrix products, arithmetic and copies ran while one was open for 3% of the time, Pallas kernels for 0%

commit v1 on v0

--- a/solution.py
+++ b/solution.py
@@ -3,6 +3,8 @@
 import jax
 import jax.numpy as jnp
 from jax import lax
+from jax.experimental import pallas as pl
+from jax.experimental.pallas import tpu as pltpu
 from jax.sharding import PartitionSpec as P
 
 QUERY_HEADS = 20
@@ -10,16 +12,246 @@
 HEAD_SIZE = 128
 DEVICE_TOKENS = 128
 PAGE_TOKENS = 16
+WIDTH = 5120
+ROWS = 2 * DEVICE_TOKENS + PAGE_TOKENS
+SIZE = {"x": 4, "y": 4, "z": 8}
+ORDERS = (("z", "x", "y"), ("y", "z", "x"), ("x", "y", "z"))
+STEPS = 8
+
+
+def place():
+    g, c = lax.axis_index("group"), lax.axis_index("ctx")
+    y_lo, core = lax.div(g, 2), lax.rem(g, 2)
+    y_hi, z, x = lax.rem(c, 2), lax.rem(lax.div(c, 2), 8), lax.div(c, 16)
+    return {"x": x, "y": y_hi * 2 + y_lo, "z": z, "core": core}
+
+
+def device(at):
+    return (
+        lax.rem(at["y"], 2) * 2 + at["core"],
+        (at["x"] * 8 + at["z"]) * 2 + lax.div(at["y"], 2),
+    )
+
+
+def moved(at, axis, by):
+    there = dict(at)
+    there[axis] = lax.rem(at[axis] + (by + SIZE[axis]), SIZE[axis])
+    return there
+
+
+def other_core(at):
+    return {**at, "core": 1 - at["core"]}
+
+
+def send(src, dst, send_sem, recv_sem, at):
+    return pltpu.make_async_remote_copy(
+        src_ref=src,
+        dst_ref=dst,
+        send_sem=send_sem,
+        recv_sem=recv_sem,
+        device_id=device(at),
+        device_id_type=pl.DeviceIdType.MESH,
+    )
+
+
+def greet(neighbours):
+    barrier = pltpu.get_barrier_semaphore()
+    for at in neighbours:
+        pl.semaphore_signal(
+            barrier, inc=1, device_id=device(at), device_id_type=pl.DeviceIdType.MESH
+        )
+    pl.semaphore_wait(barrier, len(neighbours))
+
+
+def ring_block(buf, me, axis, done, position, half):
+    def pick(name):
+        if name == axis:
+            return position
+        return None if name in done else me[name]
+
+    x, y, z = pick("x"), pick("y"), pick("z")
+    everything = slice(None)
+    y_lo = everything if y is None else lax.rem(y, 2)
+    y_hi = everything if y is None else lax.div(y, 2)
+    core = everything if half is None else half
+    return buf.at[
+        y_lo, core, everything if x is None else x, everything if z is None else z, y_hi
+    ]
+
+
+def ring_plan(order):
+    plan = []
+    for number, axis in enumerate(order):
+        for step in range(1, SIZE[axis] // 2 + 1):
+            plan.append((axis, order[:number], step))
+    return plan
+
+
+def project_kernel(
+    w_ref, hidden_ref, pool_ref, out_ref,
+    ga, gb, gc, rem_ref, rows_ref, perm_ref, main_ref, tail_ref, wide_ref,
+    ring_send, ring_recv, pair_send, pair_recv, local_sem,
+):
+    me = place()
+    core = me["core"]
+    mate = other_core(me)
+    y_lo, y_hi = lax.rem(me["y"], 2), lax.div(me["y"], 2)
+    greet([mate] + [moved(me, axis, by) for axis in "xyz" for by in (1, -1)])
+
+    def slot(buf, of_core):
+        return buf.at[y_lo, of_core, me["x"], me["z"], y_hi]
+
+    rest = w_ref[16:20, :].astype(jnp.float32)
+    for half in range(2):
+        pieces = []
+        for row in range(4):
+            for block in range(4):
+                first = (block // 2) * 512 + half * 256 + (block % 2) * 128
+                pieces.append(rest[row:row + 1, first:first + 128])
+        rem_ref[half] = jnp.concatenate(pieces, axis=0).astype(jnp.bfloat16)
+
+    def shard_parts(half):
+        return (
+            w_ref.at[pl.ds(0, 16), pl.ds(pl.multiple_of(half * 256, 128), 256)],
+            w_ref.at[pl.ds(0, 16), pl.ds(pl.multiple_of(512 + half * 256, 128), 256)],
+            rem_ref.at[half],
+        )
+
+    bufs = (ga, gb, gc)
+    own_rows = pl.ds(pl.multiple_of(core * 128, 128), 128)
+    to_mate = [
+        send(src, slot(buf, core), pair_send.at[n], pair_recv.at[n], mate)
+        for n, (src, buf) in enumerate(zip(shard_parts(1 - core), bufs))
+    ]
+    stay = [
+        pltpu.make_async_copy(src, slot(buf, core), local_sem.at[n])
+        for n, (src, buf) in enumerate(zip(shard_parts(core), bufs))
+    ]
+    for copy in to_mate + stay:
+        copy.start()
+    rows_out = send(hidden_ref, rows_ref.at[own_rows], pair_send.at[3], pair_recv.at[3], mate)
+    rows_stay = pltpu.make_async_copy(hidden_ref, rows_ref.at[own_rows], local_sem.at[3])
+    pool_stay = pltpu.make_async_copy(pool_ref, rows_ref.at[pl.ds(256, 16)], local_sem.at[4])
+    rows_stay.start()
+    pool_stay.start()
+    for copy in to_mate:
+        copy.wait_recv()
+    for copy in stay:
+        copy.wait()
+
+    plans = [ring_plan(order) for order in ORDERS]
+
+    def ring_copies(part, number):
+        axis, done, step = plans[part][number]
+        size = SIZE[axis]
+        copies = []
+        for way, sign in enumerate((1, -1)):
+            half = way if step == size // 2 else None
+            out_at = lax.rem(me[axis] + (size - sign * (step - 1)), size)
+            src = ring_block(bufs[part], me, axis, done, out_at, half)
+            copies.append(
+                send(
+                    src, src, ring_send.at[part, number, way], ring_recv.at[part, number, way],
+                    moved(me, axis, sign),
+                )
+            )
+        return copies
+
+    for number in range(STEPS):
+        for part in range(3):
+            if number > 0:
+                for copy in ring_copies(part, number - 1):
+                    copy.wait_recv()
+            for copy in ring_copies(part, number):
+                copy.start()
+        if number == 0:
+            rows_out.start()
+
+    row = lax.broadcasted_iota(jnp.int32, (640, 640), 0)
+    col = lax.broadcasted_iota(jnp.int32, (640, 640), 1)
+    tail = col - 512
+    source = jnp.where(
+        col < 512,
+        20 * lax.shift_right_logical(col, 4) + (col & 15),
+        20 * lax.shift_right_logical(tail, 2) + 16 + (tail & 3),
+    )
+    perm_ref[...] = jnp.where(row == source, 1.0, 0.0).astype(jnp.bfloat16)
+    rows_stay.wait()
+    pool_stay.wait()
+    rows_out.wait_recv()
+
+    def reorder(number, carry):
+        block = rows_ref[:, pl.ds(pl.multiple_of(number * 640, 128), 640)]
+        turned = jnp.dot(block, perm_ref[...], preferred_element_type=jnp.float32)
+        turned = turned.astype(jnp.bfloat16)
+        main_ref[:, pl.ds(pl.multiple_of(number * 512, 128), 512)] = turned[:, :512]
+        tail_ref[:, pl.ds(pl.multiple_of(number * 128, 128), 128)] = turned[:, 512:]
+        return carry
+
+    lax.fori_loop(0, 8, reorder, 0)
+
+    for copy in ring_copies(2, STEPS - 1):
+        copy.wait_recv()
+    wide_ref[...] = gc[...].reshape(4096, 128).astype(jnp.float32)
+    rest = [
+        wide_ref[pl.ds(block, 1024, stride=4), :].astype(jnp.bfloat16) for block in range(4)
+    ]
+    for part in range(2):
+        for copy in ring_copies(part, STEPS - 1):
+            copy.wait_recv()
+        both = jnp.concatenate(rest[2 * part:2 * part + 2], axis=1)
+        total = jnp.dot(
+            main_ref[...], bufs[part][...].reshape(4096, 256), preferred_element_type=jnp.float32
+        )
+        total = total + jnp.dot(tail_ref[...], both, preferred_element_type=jnp.float32)
+        out_ref[:, 256 * part:256 * part + 256] = total.astype(jnp.bfloat16)
+
+    for copy in to_mate:
+        copy.wait_send()
+    rows_out.wait_send()
+    for number in range(STEPS):
+        for part in range(3):
+            for copy in ring_copies(part, number):
+                copy.wait_send()
+
+
+def project(weight, hidden, pool):
+    return pl.pallas_call(
+        project_kernel,
+        name="project",
+        out_shape=jax.ShapeDtypeStruct((ROWS, 512), jnp.bfloat16),
+        in_specs=[
+            pl.BlockSpec(memory_space=pltpu.VMEM),
+            pl.BlockSpec(memory_space=pl.ANY),
+            pl.BlockSpec(memory_space=pl.ANY),
+        ],
+        out_specs=pl.BlockSpec(memory_space=pltpu.VMEM),
+        scratch_shapes=[
+            pltpu.VMEM((2, 2, 4, 8, 2, 16, 256), jnp.bfloat16),
+            pltpu.VMEM((2, 2, 4, 8, 2, 16, 256), jnp.bfloat16),
+            pltpu.VMEM((2, 2, 4, 8, 2, 16, 128), jnp.bfloat16),
+            pltpu.VMEM((2, 16, 128), jnp.bfloat16),
+            pltpu.VMEM((ROWS, WIDTH), jnp.bfloat16),
+            pltpu.VMEM((640, 640), jnp.bfloat16),
+            pltpu.VMEM((ROWS, 4096), jnp.bfloat16),
+            pltpu.VMEM((ROWS, 1024), jnp.bfloat16),
+            pltpu.VMEM((4096, 128), jnp.float32),
+            pltpu.SemaphoreType.DMA((3, STEPS, 2)),
+            pltpu.SemaphoreType.DMA((3, STEPS, 2)),
+            pltpu.SemaphoreType.DMA((4,)),
+            pltpu.SemaphoreType.DMA((4,)),
+            pltpu.SemaphoreType.DMA((5,)),
+        ],
+        compiler_params=pltpu.CompilerParams(
+            collective_id=0, has_side_effects=True, vmem_limit_bytes=56 * 1024 * 1024
+        ),
+    )(weight, hidden, pool)
 
 
 def passed_along(block, axis, distance):
     devices = range(lax.axis_size(axis))
     route = [(i - distance, i) for i in devices if i - distance in devices]
     return lax.ppermute(block, axis, route)
-
-
-def apply_projection(rows, weight):
-    return jnp.dot(rows, weight, preferred_element_type=jnp.float32).astype(jnp.bfloat16)
 
 
 def response_ids(lengths, positions):
@@ -50,11 +282,16 @@
 def body(hidden, queries, key_value_weight, pooled_hidden_states, group_page_table, resp_lengths):
     column_width = KEY_VALUE_HEADS * HEAD_SIZE
     scale = 1.0 / math.sqrt(HEAD_SIZE)
-    full_weight = lax.all_gather(key_value_weight, ("group", "ctx"), axis=0, tiled=True)
-    own_kv = apply_projection(hidden[0], full_weight)
-    pooled_key_value = apply_projection(
-        pooled_hidden_states.reshape(-1, pooled_hidden_states.shape[2]), full_weight
-    )
+    half = project(key_value_weight, hidden[0], pooled_hidden_states[0])
+    core = lax.rem(lax.axis_index("group"), 2)
+    swap = [(i, i ^ 1) for i in range(4)]
+    mine = lax.dynamic_slice_in_dim(half, core * 128, 128, 0)
+    theirs = lax.dynamic_slice_in_dim(half, (1 - core) * 128, 128, 0)
+    mine = jnp.concatenate([mine, half[256:]], axis=0)
+    other = lax.ppermute(jnp.concatenate([theirs, half[256:]], axis=0), "group", swap)
+    low, high = jnp.where(core == 0, mine, other), jnp.where(core == 0, other, mine)
+    both = jnp.concatenate([low[:, :256], high[:, :256], low[:, 256:], high[:, 256:]], axis=1)
+    own_kv, pooled_key_value = both[:128], both[128:]
     pool_all = lax.all_gather(pooled_key_value, "ctx", axis=0, tiled=True).reshape(
         -1, PAGE_TOKENS, 2 * column_width
     )

time: 1160 us -> 453 us (0.39)
  waiting for transfers between devices: 995 us -> 292 us
  Pallas kernels: 0 us -> 52.6 us
  other arithmetic: 33.3 us -> 10.8 us
  local copies, waits for them, and re-layouts: 44.9 us -> 23.8 us
  matrix products: 39.3 us -> 24.7 us
    all_gather x1 -> x0, waiting for transfers between devices: 724 us -> none  [body(): lax.all_gather(key_value_weight, ('group', 'ctx'), axis=0, tiled=True)]
    pallas_call x0 -> x1, Pallas kernels: none -> 52.6 us  [project(): pl.pallas_call(project_kernel, name='project', out_shape=jax.ShapeDtypeSt...]
    ppermute x16, waiting for transfers between devices: 159 us -> 179 us  [passed_along(): return lax.ppermute(block, axis, route)]
    unnamed x32 -> x13, local copies, waits for them, and re-layouts: 20.2 us -> 2.94 us
    dot_general x2 -> x0, matrix products: 11.6 us -> none  [apply_projection(): jnp.dot(rows, weight, preferred_element_type=jnp.float32)]
  transfers between devices with their start and end apart: 18 -> 18, of which waited for: 18 -> 18; matrix products, arithmetic and copies ran while one was open for 3% -> 1% of each run, Pallas kernels for 0% -> 0%
where the time goes in v1:
time: 453 us; the launch traced here: 451 us
  waiting for transfers between devices  292 us (64%)
  Pallas kernels  52.6 us (12%)
  starting transfers between devices  32 us (7%)
  matrix products  24.7 us (5%)
  local copies, waits for them, and re-layouts  23.8 us (5%)
  between operations  13.7 us (3%)
  other arithmetic  10.8 us (2%)
    ppermute x16, waiting for transfers between devices, passed_along(): return lax.ppermute(block, axis, route)  179 us
    all_gather x1, waiting for transfers between devices, body(): lax.all_gather(pooled_key_value, 'ctx', axis=0, tiled=True)  112 us
    pallas_call x1, Pallas kernels, project(): pl.pallas_call(project_kernel, name='project', out_shape=jax.ShapeDtypeSt...  52.6 us
    ppermute x16, starting transfers between devices, passed_along(): return lax.ppermute(block, axis, route)  31.9 us
    dot_general x18, matrix products, absorb(): jnp.einsum('grqk,kgd->grqd', weights.astype(jnp.bfloat16), value_rows, pr...  16.6 us
    while x32, local copies, waits for them, and re-layouts  11.4 us
  transfers between devices with their start and end apart: 18, of which 18 were waited for; matrix products, arithmetic and copies ran while one was open for 1% of the time, Pallas kernels for 0%

profile of v1, /device:TPU:14, one launch (start us, length us, event | category | flops | bytes accessed | tf_op | source)
XLA Modules:
  0.0 451.3 jit_solution(3302016326240596364)
XLA Ops:
  6.5 52.6 %project.1 = bf16[272,512]{1,0:T(8,128)(2,1)} custom-call(bf16[20,1024]{1,0:T(8,128)(2,1)} %w_ref.1, bf16[128,5120]{1,0:T(8,128)(2,1)} %bitcast.89, bf16[16,5120]{1,0:T(8,128)(2,1)} %bitcast.93), custom_call_target="tpu_custom_call" | custom-call | tf_op jit(solution)/shard_map/project/pallas_call | solution.py:219
  66.0 112.0 %all-gather.2.cloned.1.call-done = bf16[1024,1024]{1,0:T(8,128)(2,1)} async-done(((bf16[16,1024]{1,0:T(8,128)(2,1)}), bf16[1024,1024]{1,0:T(8,128)(2,1)}) %all-gather.2.cloned.1.call-update) | async-done | bytes 2097168 | tf_op jit(solution)/shard_map/all_gather | solution.py:295
  178.0 3.2 gather_fusion
  188.5 3.6 fusion.20
  192.6 250.3 %while.23 = (s32[]{:T(128)}, bf16[128,1024]{0,1:T(8,128)(2,1)}, f32[4,5,128]{2,1,0:T(8,128)S(1)}, f32[4,5,128]{2,1,0:T(8,128)S(1)}, f32[4,5,128,128]{3,2,1,0:T(8...) while((s32[]{:T(128)}, bf16[128,1024]{0,1:T(8,128)(2,1)}, ...), condition=%wide.region_11.12_spmd.clone.clone, body=%wide.region_7.11_spmd.clone.clone.sunk | while | flops 170795392 | bytes 9769433 | solution.py:348
  192.6 3.3 collective-permute-start
  196.1 9.4 %collective-permute-done = bf16[128,1024]{0,1:T(8,128)(2,1)S(1)} collective-permute-done((bf16[128,1024]{0,1:T(8,128)(2,1)}, bf16[128,1024]{0,1:T(8,128)(2,1)S(1)}, u32[]{:S(2)}, u32[]{:S(2)}) %collective-permute-start) | collective-permute-done | bytes 262176 | tf_op jit(solution)/shard_map/while/body/eval_jaxpr/ppermute | solution.py:254
  207.8 1.9 collective-permute-start
  209.9 10.8 %collective-permute-done = bf16[128,1024]{0,1:T(8,128)(2,1)S(1)} collective-permute-done((bf16[128,1024]{0,1:T(8,128)(2,1)}, bf16[128,1024]{0,1:T(8,128)(2,1)S(1)}, u32[]{:S(2)}, u32[]{:S(2)}) %collective-permute-start) | collective-permute-done | bytes 262176 | tf_op jit(solution)/shard_map/while/body/eval_jaxpr/ppermute | solution.py:254
  223.0 1.9 collective-permute-start
  225.1 10.8 %collective-permute-done = bf16[128,1024]{0,1:T(8,128)(2,1)S(1)} collective-permute-done((bf16[128,1024]{0,1:T(8,128)(2,1)}, bf16[128,1024]{0,1:T(8,128)(2,1)S(1)}, u32[]{:S(2)}, u32[]{:S(2)}) %collective-permute-start) | collective-permute-done | bytes 262176 | tf_op jit(solution)/shard_map/while/body/eval_jaxpr/ppermute | solution.py:254
  240.3 10.8 %collective-permute-done = bf16[128,1024]{0,1:T(8,128)(2,1)S(1)} collective-permute-done((bf16[128,1024]{0,1:T(8,128)(2,1)}, bf16[128,1024]{0,1:T(8,128)(2,1)S(1)}, u32[]{:S(2)}, u32[]{:S(2)}) %collective-permute-start) | collective-permute-done | bytes 262176 | tf_op jit(solution)/shard_map/while/body/eval_jaxpr/ppermute | solution.py:254
  255.5 10.8 %collective-permute-done = bf16[128,1024]{0,1:T(8,128)(2,1)S(1)} collective-permute-done((bf16[128,1024]{0,1:T(8,128)(2,1)}, bf16[128,1024]{0,1:T(8,128)(2,1)S(1)}, u32[]{:S(2)}, u32[]{:S(2)}) %collective-permute-start) | collective-permute-done | bytes 262176 | tf_op jit(solution)/shard_map/while/body/eval_jaxpr/ppermute | solution.py:254
  270.7 10.8 %collective-permute-done = bf16[128,1024]{0,1:T(8,128)(2,1)S(1)} collective-permute-done((bf16[128,1024]{0,1:T(8,128)(2,1)}, bf16[128,1024]{0,1:T(8,128)(2,1)S(1)}, u32[]{:S(2)}, u32[]{:S(2)}) %collective-permute-start) | collective-permute-done | bytes 262176 | tf_op jit(solution)/shard_map/while/body/eval_jaxpr/ppermute | solution.py:254
  285.9 11.0 %collective-permute-done = bf16[128,1024]{0,1:T(8,128)(2,1)S(1)} collective-permute-done((bf16[128,1024]{0,1:T(8,128)(2,1)}, bf16[128,1024]{0,1:T(8,128)(2,1)S(1)}, u32[]{:S(2)}, u32[]{:S(2)}) %collective-permute-start) | collective-permute-done | bytes 262176 | tf_op jit(solution)/shard_map/while/body/eval_jaxpr/ppermute | solution.py:254
  301.2 12.1 %collective-permute-done = bf16[128,1024]{0,1:T(8,128)(2,1)S(1)} collective-permute-done((bf16[128,1024]{0,1:T(8,128)(2,1)}, bf16[128,1024]{0,1:T(8,128)(2,1)S(1)}, u32[]{:S(2)}, u32[]{:S(2)}) %collective-permute-start) | collective-permute-done | bytes 262176 | tf_op jit(solution)/shard_map/while/body/eval_jaxpr/ppermute | solution.py:254
  317.7 13.3 %collective-permute-done = bf16[128,1024]{0,1:T(8,128)(2,1)S(1)} collective-permute-done((bf16[128,1024]{0,1:T(8,128)(2,1)}, bf16[128,1024]{0,1:T(8,128)(2,1)S(1)}, u32[]{:S(2)}, u32[]{:S(2)}) %collective-permute-start) | collective-permute-done | bytes 262176 | tf_op jit(solution)/shard_map/while/body/eval_jaxpr/ppermute | solution.py:254
  335.4 12.8 %collective-permute-done = bf16[128,1024]{0,1:T(8,128)(2,1)S(1)} collective-permute-done((bf16[128,1024]{0,1:T(8,128)(2,1)}, bf16[128,1024]{0,1:T(8,128)(2,1)S(1)}, u32[]{:S(2)}, u32[]{:S(2)}) %collective-permute-start) | collective-permute-done | bytes 262176 | tf_op jit(solution)/shard_map/while/body/eval_jaxpr/ppermute | solution.py:254
  352.5 12.0 %collective-permute-done = bf16[128,1024]{0,1:T(8,128)(2,1)S(1)} collective-permute-done((bf16[128,1024]{0,1:T(8,128)(2,1)}, bf16[128,1024]{0,1:T(8,128)(2,1)S(1)}, u32[]{:S(2)}, u32[]{:S(2)}) %collective-permute-start) | collective-permute-done | bytes 262176 | tf_op jit(solution)/shard_map/while/body/eval_jaxpr/ppermute | solution.py:254
  368.8 11.0 %collective-permute-done = bf16[128,1024]{0,1:T(8,128)(2,1)S(1)} collective-permute-done((bf16[128,1024]{0,1:T(8,128)(2,1)}, bf16[128,1024]{0,1:T(8,128)(2,1)S(1)}, u32[]{:S(2)}, u32[]{:S(2)}) %collective-permute-start) | collective-permute-done | bytes 262176 | tf_op jit(solution)/shard_map/while/body/eval_jaxpr/ppermute | solution.py:254
  384.2 10.8 %collective-permute-done = bf16[128,1024]{0,1:T(8,128)(2,1)S(1)} collective-permute-done((bf16[128,1024]{0,1:T(8,128)(2,1)}, bf16[128,1024]{0,1:T(8,128)(2,1)S(1)}, u32[]{:S(2)}, u32[]{:S(2)}) %collective-permute-start) | collective-permute-done | bytes 262176 | tf_op jit(solution)/shard_map/while/body/eval_jaxpr/ppermute | solution.py:254
  399.4 10.8 %collective-permute-done = bf16[128,1024]{0,1:T(8,128)(2,1)S(1)} collective-permute-done((bf16[128,1024]{0,1:T(8,128)(2,1)}, bf16[128,1024]{0,1:T(8,128)(2,1)S(1)}, u32[]{:S(2)}, u32[]{:S(2)}) %collective-permute-start) | collective-permute-done | bytes 262176 | tf_op jit(solution)/shard_map/while/body/eval_jaxpr/ppermute | solution.py:254
  414.6 10.8 %collective-permute-done = bf16[128,1024]{0,1:T(8,128)(2,1)S(1)} collective-permute-done((bf16[128,1024]{0,1:T(8,128)(2,1)}, bf16[128,1024]{0,1:T(8,128)(2,1)S(1)}, u32[]{:S(2)}, u32[]{:S(2)}) %collective-permute-start) | collective-permute-done | bytes 262176 | tf_op jit(solution)/shard_map/while/body/eval_jaxpr/ppermute | solution.py:254
  429.8 10.8 %collective-permute-done = bf16[128,1024]{0,1:T(8,128)(2,1)S(1)} collective-permute-done((bf16[128,1024]{0,1:T(8,128)(2,1)}, bf16[128,1024]{0,1:T(8,128)(2,1)S(1)}, u32[]{:S(2)}, u32[]{:S(2)}) %collective-permute-start) | collective-permute-done | bytes 262176 | tf_op jit(solution)/shard_map/while/body/eval_jaxpr/ppermute | solution.py:254
  (259 shorter events, 78.8 us)
Async XLA Ops:
  6.5 171.5 %all-gather.2.cloned.1.call-start = ((), (), s32[]{:S(2)}) async-start(), calls=%async_computation | async-start | bytes 2129920 | tf_op jit(solution)/shard_map/all_gather | solution.py:295
  59.1 4.0 copy-start.4
  59.1 4.2 copy-start.2
  60.9 1.5 collective-permute-start.1
  62.4 1.3 copy-start.3
  185.8 2.3 copy-start
  185.8 2.3 copy-start.1
  192.6 13.0 %collective-permute-start = (bf16[128,1024]{0,1:T(8,128)(2,1)}, bf16[128,1024]{0,1:T(8,128)(2,1)S(1)}, u32[]{:S(2)}, u32[]{:S(2)}) collective-permute-start(bf16[128,1024]{0,1:T(8,128)(2,1)} %get-tuple-element.441), channel_id=1, source_target_pairs={{0,1},{1,2},{2,3},{3,4},{4,5},{5,6},{6,7},{7,8},{8,9},{9,10},{10,1... | collective-permute-start | bytes 786440 | tf_op jit(solution)/shard_map/while/body/eval_jaxpr/ppermute | solution.py:254
  207.8 13.0 %collective-permute-start = (bf16[128,1024]{0,1:T(8,128)(2,1)}, bf16[128,1024]{0,1:T(8,128)(2,1)S(1)}, u32[]{:S(2)}, u32[]{:S(2)}) collective-permute-start(bf16[128,1024]{0,1:T(8,128)(2,1)} %get-tuple-element.441), channel_id=1, source_target_pairs={{0,1},{1,2},{2,3},{3,4},{4,5},{5,6},{6,7},{7,8},{8,9},{9,10},{10,1... | collective-permute-start | bytes 786440 | tf_op jit(solution)/shard_map/while/body/eval_jaxpr/ppermute | solution.py:254
  223.0 13.0 %collective-permute-start = (bf16[128,1024]{0,1:T(8,128)(2,1)}, bf16[128,1024]{0,1:T(8,128)(2,1)S(1)}, u32[]{:S(2)}, u32[]{:S(2)}) collective-permute-start(bf16[128,1024]{0,1:T(8,128)(2,1)} %get-tuple-element.441), channel_id=1, source_target_pairs={{0,1},{1,2},{2,3},{3,4},{4,5},{5,6},{6,7},{7,8},{8,9},{9,10},{10,1... | collective-permute-start | bytes 786440 | tf_op jit(solution)/shard_map/while/body/eval_jaxpr/ppermute | solution.py:254
  238.2 13.0 %collective-permute-start = (bf16[128,1024]{0,1:T(8,128)(2,1)}, bf16[128,1024]{0,1:T(8,128)(2,1)S(1)}, u32[]{:S(2)}, u32[]{:S(2)}) collective-permute-start(bf16[128,1024]{0,1:T(8,128)(2,1)} %get-tuple-element.441), channel_id=1, source_target_pairs={{0,1},{1,2},{2,3},{3,4},{4,5},{5,6},{6,7},{7,8},{8,9},{9,10},{10,1... | collective-permute-start | bytes 786440 | tf_op jit(solution)/shard_map/while/body/eval_jaxpr/ppermute | solution.py:254
  253.3 13.0 %collective-permute-start = (bf16[128,1024]{0,1:T(8,128)(2,1)}, bf16[128,1024]{0,1:T(8,128)(2,1)S(1)}, u32[]{:S(2)}, u32[]{:S(2)}) collective-permute-start(bf16[128,1024]{0,1:T(8,128)(2,1)} %get-tuple-element.441), channel_id=1, source_target_pairs={{0,1},{1,2},{2,3},{3,4},{4,5},{5,6},{6,7},{7,8},{8,9},{9,10},{10,1... | collective-permute-start | bytes 786440 | tf_op jit(solution)/shard_map/while/body/eval_jaxpr/ppermute | solution.py:254
  268.5 13.0 %collective-permute-start = (bf16[128,1024]{0,1:T(8,128)(2,1)}, bf16[128,1024]{0,1:T(8,128)(2,1)S(1)}, u32[]{:S(2)}, u32[]{:S(2)}) collective-permute-start(bf16[128,1024]{0,1:T(8,128)(2,1)} %get-tuple-element.441), channel_id=1, source_target_pairs={{0,1},{1,2},{2,3},{3,4},{4,5},{5,6},{6,7},{7,8},{8,9},{9,10},{10,1... | collective-permute-start | bytes 786440 | tf_op jit(solution)/shard_map/while/body/eval_jaxpr/ppermute | solution.py:254
  283.7 13.2 %collective-permute-start = (bf16[128,1024]{0,1:T(8,128)(2,1)}, bf16[128,1024]{0,1:T(8,128)(2,1)S(1)}, u32[]{:S(2)}, u32[]{:S(2)}) collective-permute-start(bf16[128,1024]{0,1:T(8,128)(2,1)} %get-tuple-element.441), channel_id=1, source_target_pairs={{0,1},{1,2},{2,3},{3,4},{4,5},{5,6},{6,7},{7,8},{8,9},{9,10},{10,1... | collective-permute-start | bytes 786440 | tf_op jit(solution)/shard_map/while/body/eval_jaxpr/ppermute | solution.py:254
  299.1 14.2 %collective-permute-start = (bf16[128,1024]{0,1:T(8,128)(2,1)}, bf16[128,1024]{0,1:T(8,128)(2,1)S(1)}, u32[]{:S(2)}, u32[]{:S(2)}) collective-permute-start(bf16[128,1024]{0,1:T(8,128)(2,1)} %get-tuple-element.441), channel_id=1, source_target_pairs={{0,1},{1,2},{2,3},{3,4},{4,5},{5,6},{6,7},{7,8},{8,9},{9,10},{10,1... | collective-permute-start | bytes 786440 | tf_op jit(solution)/shard_map/while/body/eval_jaxpr/ppermute | solution.py:254
  315.5 15.5 %collective-permute-start = (bf16[128,1024]{0,1:T(8,128)(2,1)}, bf16[128,1024]{0,1:T(8,128)(2,1)S(1)}, u32[]{:S(2)}, u32[]{:S(2)}) collective-permute-start(bf16[128,1024]{0,1:T(8,128)(2,1)} %get-tuple-element.441), channel_id=1, source_target_pairs={{0,1},{1,2},{2,3},{3,4},{4,5},{5,6},{6,7},{7,8},{8,9},{9,10},{10,1... | collective-permute-start | bytes 786440 | tf_op jit(solution)/shard_map/while/body/eval_jaxpr/ppermute | solution.py:254
  333.2 14.9 %collective-permute-start = (bf16[128,1024]{0,1:T(8,128)(2,1)}, bf16[128,1024]{0,1:T(8,128)(2,1)S(1)}, u32[]{:S(2)}, u32[]{:S(2)}) collective-permute-start(bf16[128,1024]{0,1:T(8,128)(2,1)} %get-tuple-element.441), channel_id=1, source_target_pairs={{0,1},{1,2},{2,3},{3,4},{4,5},{5,6},{6,7},{7,8},{8,9},{9,10},{10,1... | collective-permute-start | bytes 786440 | tf_op jit(solution)/shard_map/while/body/eval_jaxpr/ppermute | solution.py:254
  350.4 14.1 %collective-permute-start = (bf16[128,1024]{0,1:T(8,128)(2,1)}, bf16[128,1024]{0,1:T(8,128)(2,1)S(1)}, u32[]{:S(2)}, u32[]{:S(2)}) collective-permute-start(bf16[128,1024]{0,1:T(8,128)(2,1)} %get-tuple-element.441), channel_id=1, source_target_pairs={{0,1},{1,2},{2,3},{3,4},{4,5},{5,6},{6,7},{7,8},{8,9},{9,10},{10,1... | collective-permute-start | bytes 786440 | tf_op jit(solution)/shard_map/while/body/eval_jaxpr/ppermute | solution.py:254
  366.7 13.2 %collective-permute-start = (bf16[128,1024]{0,1:T(8,128)(2,1)}, bf16[128,1024]{0,1:T(8,128)(2,1)S(1)}, u32[]{:S(2)}, u32[]{:S(2)}) collective-permute-start(bf16[128,1024]{0,1:T(8,128)(2,1)} %get-tuple-element.441), channel_id=1, source_target_pairs={{0,1},{1,2},{2,3},{3,4},{4,5},{5,6},{6,7},{7,8},{8,9},{9,10},{10,1... | collective-permute-start | bytes 786440 | tf_op jit(solution)/shard_map/while/body/eval_jaxpr/ppermute | solution.py:254
  382.1 13.0 %collective-permute-start = (bf16[128,1024]{0,1:T(8,128)(2,1)}, bf16[128,1024]{0,1:T(8,128)(2,1)S(1)}, u32[]{:S(2)}, u32[]{:S(2)}) collective-permute-start(bf16[128,1024]{0,1:T(8,128)(2,1)} %get-tuple-element.441), channel_id=1, source_target_pairs={{0,1},{1,2},{2,3},{3,4},{4,5},{5,6},{6,7},{7,8},{8,9},{9,10},{10,1... | collective-permute-start | bytes 786440 | tf_op jit(solution)/shard_map/while/body/eval_jaxpr/ppermute | solution.py:254
  397.3 13.0 %collective-permute-start = (bf16[128,1024]{0,1:T(8,128)(2,1)}, bf16[128,1024]{0,1:T(8,128)(2,1)S(1)}, u32[]{:S(2)}, u32[]{:S(2)}) collective-permute-start(bf16[128,1024]{0,1:T(8,128)(2,1)} %get-tuple-element.441), channel_id=1, source_target_pairs={{0,1},{1,2},{2,3},{3,4},{4,5},{5,6},{6,7},{7,8},{8,9},{9,10},{10,1... | collective-permute-start | bytes 786440 | tf_op jit(solution)/shard_map/while/body/eval_jaxpr/ppermute | solution.py:254
  412.5 13.0 %collective-permute-start = (bf16[128,1024]{0,1:T(8,128)(2,1)}, bf16[128,1024]{0,1:T(8,128)(2,1)S(1)}, u32[]{:S(2)}, u32[]{:S(2)}) collective-permute-start(bf16[128,1024]{0,1:T(8,128)(2,1)} %get-tuple-element.441), channel_id=1, source_target_pairs={{0,1},{1,2},{2,3},{3,4},{4,5},{5,6},{6,7},{7,8},{8,9},{9,10},{10,1... | collective-permute-start | bytes 786440 | tf_op jit(solution)/shard_map/while/body/eval_jaxpr/ppermute | solution.py:254
  427.6 13.0 %collective-permute-start = (bf16[128,1024]{0,1:T(8,128)(2,1)}, bf16[128,1024]{0,1:T(8,128)(2,1)S(1)}, u32[]{:S(2)}, u32[]{:S(2)}) collective-permute-start(bf16[128,1024]{0,1:T(8,128)(2,1)} %get-tuple-element.441), channel_id=1, source_target_pairs={{0,1},{1,2},{2,3},{3,4},{4,5},{5,6},{6,7},{7,8},{8,9},{9,10},{10,1... | collective-permute-start | bytes 786440 | tf_op jit(solution)/shard_map/while/body/eval_jaxpr/ppermute | solution.py:254
Sparse Core Ops, SparseCore 0:
  63.2 114.7 all-gather.1

commit v2 on v1

--- a/solution.py
+++ b/solution.py
@@ -248,110 +248,293 @@
     )(weight, hidden, pool)
 
 
-def passed_along(block, axis, distance):
-    devices = range(lax.axis_size(axis))
-    route = [(i - distance, i) for i in devices if i - distance in devices]
-    return lax.ppermute(block, axis, route)
-
-
-def response_ids(lengths, positions):
-    ends = jnp.cumsum(lengths)
-    return jnp.sum((positions[:, None] >= ends[None, :]).astype(jnp.int32), axis=1)
-
-
-def absorb(state, query_matrix, key_rows, value_rows, live, scale):
-    top, total, accum = state
-    scores = (
-        jnp.einsum("qgrd,kgd->grqk", query_matrix, key_rows, preferred_element_type=jnp.float32)
-        * scale
-    )
-    scores = jnp.where(live[None, None], scores, -jnp.inf)
-    new_top = jnp.maximum(top, jnp.max(scores, axis=3))
-    factor = jnp.exp(top - new_top)
-    weights = jnp.exp(scores - new_top[..., None])
-    total = total * factor + jnp.sum(weights, axis=3)
-    accum = accum * factor[..., None] + jnp.einsum(
-        "grqk,kgd->grqd",
-        weights.astype(jnp.bfloat16),
-        value_rows,
-        preferred_element_type=jnp.float32,
-    )
-    return (new_top, total, accum)
+SCALE = math.log2(math.e) / math.sqrt(HEAD_SIZE)
+HALF_HEADS = QUERY_HEADS // 2
+HALF_WIDTH = HALF_HEADS * HEAD_SIZE
+PAIR = 2 * DEVICE_TOKENS
+
+
+def along(me, by):
+    at = lax.rem(me["x"] * 8 + me["z"] + (32 + by), 32)
+    return {**me, "x": lax.div(at, 8), "z": lax.rem(at, 8)}
+
+
+def slot_of(back):
+    return 0 if back == 0 else 2 * back - 1 if back <= 4 else 2 * (9 - back)
+
+
+def attend_kernel(
+    half_ref, queries_ref, pages_ref, lengths_ref, out_ref,
+    kv_ref, pool_ref, query_ref, give_ref, bias_ref, top_ref, total_ref, sum_ref,
+    group_send, group_recv, query_send, query_recv, local_sem,
+    halo_send, halo_recv, pool_send, pool_recv, give_send, give_recv,
+):
+    me = place()
+    core = me["core"]
+    y_lo, y_hi = lax.rem(me["y"], 2), lax.div(me["y"], 2)
+    pair = me["x"] * 8 + me["z"]
+    partner = {**me, "y": (1 - y_hi) * 2 + y_lo}
+    greet(
+        [other_core(me), partner, other_core(partner), along(me, 1), along(me, -1)]
+        + [moved(me, axis, by) for axis in "xz" for by in (1, -1)]
+    )
+
+    def half_columns(ref, of):
+        return ref.at[:, pl.ds(pl.multiple_of(of * HALF_WIDTH, 128), HALF_WIDTH)]
+
+    query_out = send(
+        half_columns(queries_ref, 1 - y_hi), query_ref.at[y_hi], query_send, query_recv, partner
+    )
+    query_stay = pltpu.make_async_copy(
+        half_columns(queries_ref, y_hi), query_ref.at[y_hi], local_sem
+    )
+
+    def regroup(to_core, what, from_hi):
+        if what == 0:
+            src = half_ref.at[pl.ds(to_core * 128, 128)]
+            dst = kv_ref.at[0, pl.ds(pl.multiple_of(from_hi * 128, 128), 128)]
+        else:
+            src = half_ref.at[pl.ds(256, 16)]
+            dst = pool_ref.at[pair * 2 + from_hi]
+        return send(
+            src, dst, group_send.at[to_core, what], group_recv.at[from_hi, what],
+            {**me, "y": core * 2 + y_lo, "core": jnp.int32(to_core)},
+        )
+
+    for what in (1, 0):
+        for to_core in range(2):
+            stays = jnp.logical_and(core == y_hi, core == to_core)
+
+            @pl.when(stays)
+            def _():
+                copy = regroup(to_core, what, y_hi)
+                pltpu.make_async_copy(copy.src_ref, copy.dst_ref, group_recv.at[y_hi, what]).start()
+
+            @pl.when(jnp.logical_not(stays))
+            def _():
+                regroup(to_core, what, y_hi).start()
+
+    query_out.start()
+    query_stay.start()
+
+    pool_plan = ring_plan(("z", "x"))
+
+    def pool_copies(number):
+        axis, _, step = pool_plan[number]
+        size = SIZE[axis]
+        copies = []
+        for way, sign in enumerate((1, -1)):
+            at = lax.rem(me[axis] + (size - sign * (step - 1)), size)
+            count = 2 if axis == "z" else 16
+            first = (me["x"] * 8 + at) * 2 if axis == "z" else at * 16
+            if step == size // 2:
+                count = count // 2
+                first = first + way * count
+            block = pool_ref.at[pl.ds(first, count)]
+            copies.append(
+                send(
+                    block, block, pool_send.at[number, way], pool_recv.at[number, way],
+                    moved(me, axis, sign),
+                )
+            )
+        return copies
+
+    def pool_step(number):
+        if number > 0:
+            for copy in pool_copies(number - 1):
+                copy.wait_recv()
+        if number < len(pool_plan):
+            for copy in pool_copies(number):
+                copy.start()
+
+    def forth(step):
+        return send(
+            kv_ref.at[slot_of(step - 1)], kv_ref.at[slot_of(step)],
+            halo_send.at[step - 1], halo_recv.at[step - 1], along(me, 1),
+        )
+
+    def back(step):
+        if step == 0:
+            src, to = kv_ref.at[slot_of(0)], moved_pair
+        else:
+            src, to = kv_ref.at[slot_of(9 - step)], along(me, -1)
+        return send(
+            src, kv_ref.at[slot_of(8 - step)], halo_send.at[4 + step], halo_recv.at[4 + step], to
+        )
+
+    moved_pair = moved(me, "x", 1)
+
+    for what in (1, 0):
+        for from_hi in range(2):
+            regroup(0, what, jnp.int32(from_hi)).wait_recv()
+        if what == 1:
+            pool_step(0)
+    forth(1).start()
+    back(0).start()
+
+    row = lax.broadcasted_iota(jnp.int32, (PAIR, PAIR), 0)
+    lane = lax.broadcasted_iota(jnp.int32, (PAIR, PAIR), 1)
+    position = pair * PAIR + row
+    begin = jnp.zeros((PAIR, PAIR), jnp.int32)
+    end = jnp.int32(0)
+    for number in range(8):
+        end = end + lengths_ref[0, number]
+        begin = jnp.where(position >= end, end, begin)
+
+    def bias_of(back_by):
+        key = (pair - back_by) * PAIR + lane
+        live = key >= begin
+        if back_by == 0:
+            live = jnp.logical_and(live, key <= position)
+        return jnp.where(live, 0.0, -jnp.inf).astype(jnp.float32)
+
+    top_ref[...] = jnp.full(top_ref.shape, -jnp.inf, jnp.float32)
+    total_ref[...] = jnp.zeros(total_ref.shape, jnp.float32)
+    sum_ref[...] = jnp.zeros(sum_ref.shape, jnp.float32)
+
+    def attend(first, count, masked, head):
+        rows = count * PAIR
+
+        def one(number, carry):
+            column = pl.multiple_of((head * 5 + number) * 128, 128)
+            at = head * 5 + number
+            query = query_ref[:, :, pl.ds(column, 128)].reshape(PAIR, 128)
+            key = kv_ref[first:first + count, :, head * 128:head * 128 + 128].reshape(rows, 128)
+            value = kv_ref[first:first + count, :, 256 + head * 128:384 + head * 128]
+            score = lax.dot_general(
+                query, key, (((1,), (1,)), ((), ())), preferred_element_type=jnp.float32
+            )
+            if masked:
+                score = score + bias_ref[:, :rows]
+            old = top_ref[at]
+            new = jnp.maximum(old, jnp.max(score, axis=1, keepdims=True))
+            factor = jnp.exp2((old - new) * SCALE)
+            weight = jnp.exp2((score - jnp.concatenate([new] * (rows // 128), axis=1)) * SCALE)
+            part = weight[:, :128]
+            for lanes in range(128, rows, 128):
+                part = part + weight[:, lanes:lanes + 128]
+            top_ref[at] = new
+            total_ref[at] = total_ref[at] * factor + part
+            sum_ref[at] = sum_ref[at] * factor + jnp.dot(
+                weight.astype(jnp.bfloat16), value.reshape(rows, 128),
+                preferred_element_type=jnp.float32,
+            )
+            return carry
+
+        lax.fori_loop(0, 5, one, 0, unroll=5)
+
+    def finish(head):
+        for number in range(5):
+            at = head * 5 + number
+            total = jnp.sum(total_ref[at], axis=1, keepdims=True)
+            done = (sum_ref[at] / total).astype(jnp.bfloat16).reshape(2, 128, 128)
+            for hi in range(2):
+                @pl.when(y_hi == hi)
+                def _():
+                    first = hi * HALF_WIDTH + at * 128
+                    out_ref[:, first:first + 128] = done[hi]
+                    give_ref[:, at * 128:at * 128 + 128] = done[1 - hi]
+
+    def give(head):
+        first = pl.multiple_of(y_hi * HALF_WIDTH + head * 640, 128)
+        return send(
+            give_ref.at[:, pl.ds(head * 640, 640)], out_ref.at[:, pl.ds(first, 640)],
+            give_send.at[head], give_recv.at[head], partner,
+        )
+
+    pool_step(1)
+    query_out.wait_recv()
+    query_stay.wait()
+    bias_ref[:, :PAIR] = bias_of(0)
+    for head in range(2):
+        attend(0, 1, True, head)
+        if head == 0:
+            pool_step(2)
+    for step in range(1, 5):
+        forth(step).wait_recv()
+        back(step - 1).wait_recv()
+        if step < 4:
+            forth(step + 1).start()
+            back(step).start()
+        if step < 4:
+            pool_step(step * 2 + 1 if step < 3 else 6)
+        bias_ref[:, :PAIR] = bias_of(step)
+        bias_ref[:, PAIR:] = bias_of(9 - step)
+        for head in range(2):
+            attend(2 * step - 1, 2, True, head)
+            if head == 0 and step < 2:
+                pool_step(step * 2 + 2)
+            if step == 4:
+                finish(head)
+                give(head).start()
+        if step == 3:
+            def page(number, carry):
+                first = pl.multiple_of(lax.rem(number, 16) * 16, 16)
+                kv_ref[9 + lax.div(number, 16), pl.ds(first, 16)] = pool_ref[pages_ref[0, number]]
+                return carry
+
+            lax.fori_loop(0, 32, page, 0)
+            for head in range(2):
+                attend(9, 2, False, head)
+
+    for head in range(2):
+        give(head).wait()
+    query_out.wait_send()
+    for what in range(2):
+        for to_core in range(2):
+            @pl.when(jnp.logical_not(jnp.logical_and(core == y_hi, core == to_core)))
+            def _():
+                regroup(to_core, what, y_hi).wait_send()
+    for number in range(len(pool_plan)):
+        for copy in pool_copies(number):
+            copy.wait_send()
+    for step in range(1, 5):
+        forth(step).wait_send()
+        back(step - 1).wait_send()
+
+
+def attend_all(half, queries, pages, lengths):
+    return pl.pallas_call(
+        attend_kernel,
+        name="attend",
+        out_shape=jax.ShapeDtypeStruct((DEVICE_TOKENS, QUERY_HEADS * HEAD_SIZE), jnp.bfloat16),
+        in_specs=[
+            pl.BlockSpec(memory_space=pltpu.VMEM),
+            pl.BlockSpec(memory_space=pl.ANY),
+            pl.BlockSpec(memory_space=pltpu.SMEM),
+            pl.BlockSpec(memory_space=pltpu.SMEM),
+        ],
+        out_specs=pl.BlockSpec(memory_space=pltpu.VMEM),
+        scratch_shapes=[
+            pltpu.VMEM((11, PAIR, 512), jnp.bfloat16),
+            pltpu.VMEM((64, PAGE_TOKENS, 512), jnp.bfloat16),
+            pltpu.VMEM((2, DEVICE_TOKENS, HALF_WIDTH), jnp.bfloat16),
+            pltpu.VMEM((DEVICE_TOKENS, HALF_WIDTH), jnp.bfloat16),
+            pltpu.VMEM((PAIR, 2 * PAIR), jnp.float32),
+            pltpu.VMEM((HALF_HEADS, PAIR, 128), jnp.float32),
+            pltpu.VMEM((HALF_HEADS, PAIR, 128), jnp.float32),
+            pltpu.VMEM((HALF_HEADS, PAIR, 128), jnp.float32),
+            pltpu.SemaphoreType.DMA((2, 2)),
+            pltpu.SemaphoreType.DMA((2, 2)),
+            pltpu.SemaphoreType.DMA,
+            pltpu.SemaphoreType.DMA,
+            pltpu.SemaphoreType.DMA,
+            pltpu.SemaphoreType.DMA((8,)),
+            pltpu.SemaphoreType.DMA((8,)),
+            pltpu.SemaphoreType.DMA((6, 2)),
+            pltpu.SemaphoreType.DMA((6, 2)),
+            pltpu.SemaphoreType.DMA((2,)),
+            pltpu.SemaphoreType.DMA((2,)),
+        ],
+        compiler_params=pltpu.CompilerParams(
+            collective_id=1, has_side_effects=True, vmem_limit_bytes=48 * 1024 * 1024
+        ),
+    )(half, queries, pages, lengths)
 
 
 def body(hidden, queries, key_value_weight, pooled_hidden_states, group_page_table, resp_lengths):
-    column_width = KEY_VALUE_HEADS * HEAD_SIZE
-    scale = 1.0 / math.sqrt(HEAD_SIZE)
     half = project(key_value_weight, hidden[0], pooled_hidden_states[0])
-    core = lax.rem(lax.axis_index("group"), 2)
-    swap = [(i, i ^ 1) for i in range(4)]
-    mine = lax.dynamic_slice_in_dim(half, core * 128, 128, 0)
-    theirs = lax.dynamic_slice_in_dim(half, (1 - core) * 128, 128, 0)
-    mine = jnp.concatenate([mine, half[256:]], axis=0)
-    other = lax.ppermute(jnp.concatenate([theirs, half[256:]], axis=0), "group", swap)
-    low, high = jnp.where(core == 0, mine, other), jnp.where(core == 0, other, mine)
-    both = jnp.concatenate([low[:, :256], high[:, :256], low[:, 256:], high[:, 256:]], axis=1)
-    own_kv, pooled_key_value = both[:128], both[128:]
-    pool_all = lax.all_gather(pooled_key_value, "ctx", axis=0, tiled=True).reshape(
-        -1, PAGE_TOKENS, 2 * column_width
-    )
-    prompt_key_value = jnp.take(pool_all, group_page_table[0], axis=0).reshape(-1, 2 * column_width)
-    lengths = resp_lengths[0]
-    query_matrix = queries[0].reshape(
-        DEVICE_TOKENS, KEY_VALUE_HEADS, QUERY_HEADS // KEY_VALUE_HEADS, HEAD_SIZE
-    )
-    first = lax.axis_index("ctx") * DEVICE_TOKENS
-    q_pos = first + jnp.arange(DEVICE_TOKENS, dtype=jnp.int32)
-    q_ids = response_ids(lengths, q_pos)
-    dimension_list = (KEY_VALUE_HEADS, QUERY_HEADS // KEY_VALUE_HEADS, DEVICE_TOKENS)
-    state = (
-        jnp.full(dimension_list, -jnp.inf, jnp.float32),
-        jnp.zeros(dimension_list, jnp.float32),
-        jnp.zeros(dimension_list + (HEAD_SIZE,), jnp.float32),
-    )
-    prompt_token_rows = prompt_key_value.shape[0]
-    prompt_live = jnp.ones((DEVICE_TOKENS, prompt_token_rows), dtype=bool)
-    state = absorb(
-        state,
-        query_matrix,
-        prompt_key_value[:, :column_width].reshape(prompt_token_rows, KEY_VALUE_HEADS, HEAD_SIZE),
-        prompt_key_value[:, column_width:].reshape(prompt_token_rows, KEY_VALUE_HEADS, HEAD_SIZE),
-        prompt_live,
-        scale,
-    )
-
-    def block_step(carry, key_value_rows, k_first):
-        count_of_rows = key_value_rows.shape[0]
-        k_pos = k_first + jnp.arange(count_of_rows, dtype=jnp.int32)
-        k_ids = response_ids(lengths, k_pos)
-        live = (
-            (k_pos[None, :] <= q_pos[:, None])
-            & (k_pos[None, :] >= 0)
-            & (k_ids[None, :] == q_ids[:, None])
-        )
-        key_rows = key_value_rows[:, :column_width].reshape(
-            count_of_rows, KEY_VALUE_HEADS, HEAD_SIZE
-        )
-        value_rows = key_value_rows[:, column_width:].reshape(
-            count_of_rows, KEY_VALUE_HEADS, HEAD_SIZE
-        )
-        return absorb(carry, query_matrix, key_rows, value_rows, live, scale)
-
-    state = block_step(state, own_kv, first)
-    reach_steps = lax.axis_size("ctx") // 4
-
-    def near_step(page_index, carry):
-        moving, inner_state = carry
-        moving = passed_along(moving, "ctx", 1)
-        return (moving, block_step(inner_state, moving, first - (page_index + 1) * DEVICE_TOKENS))
-
-    state = lax.fori_loop(0, reach_steps, near_step, (own_kv, state))[1]
-    mixed = state[2] / state[1][..., None]
-    return (
-        jnp.transpose(mixed, (2, 0, 1, 3))
-        .reshape(1, DEVICE_TOKENS, QUERY_HEADS * HEAD_SIZE)
-        .astype(jnp.bfloat16)
-    )
+    return attend_all(half, queries[0], group_page_table, resp_lengths)[None]
 
 
 def solution(mesh):

time: 453 us -> 131 us (0.29)
  waiting for transfers between devices: 292 us -> 0 us
  Pallas kernels: 52.6 us -> 129 us
  starting transfers between devices: 32 us -> 0 us
  matrix products: 24.7 us -> 0 us
  local copies, waits for them, and re-layouts: 23.8 us -> 1.8 us
  between operations: 13.7 us -> 0.05 us
  other arithmetic: 10.8 us -> 0 us
    ppermute x17 -> x0, waiting for transfers between devices: 180 us -> none  [the longest x16 179 us: passed_along(): return lax.ppermute(block, axis, route)]
    all_gather x1 -> x0, waiting for transfers between devices: 112 us -> none  [body(): lax.all_gather(pooled_key_value, 'ctx', axis=0, tiled=True)]
    pallas_call x0 -> x1, Pallas kernels: none -> 76.5 us  [attend_all(): pl.pallas_call(attend_kernel, name='attend', out_shape=jax.ShapeDtypeStru...]
    ppermute x17 -> x0, starting transfers between devices: 32 us -> none  [the longest x16 31.9 us: passed_along(): return lax.ppermute(block, axis, route)]
    dot_general x36 -> x0, matrix products: 24.7 us -> none  [the longest x18 16.6 us: absorb(): jnp.einsum('grqk,kgd->grqd', weights.astype(jnp.bfloat16), value_rows, pr...]
    while x33 -> x0, local copies, waits for them, and re-layouts: 11.8 us -> none
    reduce_sum x35 -> x0, other arithmetic: 5.65 us -> none  [the longest x18 4.21 us: absorb(): total = total * factor + jnp.sum(weights, axis=3)]
  transfers between devices with their start and end apart: 18 -> 0, of which waited for: 18 -> 0; matrix products, arithmetic and copies ran while one was open for 1% -> 0% of each run, Pallas kernels for 0% -> 0%
where the time goes in v2:
time: 131 us
  Pallas kernels  129 us (98%)
  local copies, waits for them, and re-layouts  1.8 us (1%)
    pallas_call x1, Pallas kernels, attend_all(): pl.pallas_call(attend_kernel, name='attend', out_shape=jax.ShapeDtypeStru...  76.5 us
    pallas_call x1, Pallas kernels, project(): pl.pallas_call(project_kernel, name='project', out_shape=jax.ShapeDtypeSt...  52.8 us

profile of v2, /device:TPU:14, one launch (start us, length us, event | category | flops | bytes accessed | tf_op | source)
XLA Modules:
  0.0 131.1 jit_solution(7966124577878478699)
XLA Ops:
  0.0 0.0 copy-start.3
  0.0 0.0 copy-start.2
  0.0 0.0 copy-start.1
  0.0 52.8 %project.1.half_ref = bf16[272,512]{1,0:T(8,128)(2,1)} custom-call(bf16[20,1024]{1,0:T(8,128)(2,1)} %w_ref.1, bf16[128,5120]{1,0:T(8,128)(2,1)} %bitcast.6, bf16[16,5120]{1,0:T(8,128)(2,1)} %bitcast.7), custom_call_target="tpu_custom_call" | custom-call | tf_op jit(solution)/shard_map/project/pallas_call | solution.py:219
  52.8 0.0 copy-done.3
  52.8 0.0 copy-done.2
  52.8 0.0 copy-done.1
  52.8 0.0 copy-start
  52.8 0.9 copy-done
  53.8 76.5 %attend.1 = bf16[128,2560]{1,0:T(8,128)(2,1)S(1)} custom-call(bf16[272,512]{1,0:T(8,128)(2,1)S(1)} %copy-done, bf16[128,2560]{1,0:T(8,128)(2,1)S(1)} %bitcast.5, s32[1,32]{1,0:T(1,128)S(1)} %copy-done.2, s32[1,8]{1,0:T(1,128)S(1)} %copy-done.3), custom_call_target="tpu_custom_call" | custom-call | tf_op jit(solution)/shard_map/attend/pallas_call | solution.py:497
  130.3 0.8 copy.8
Async XLA Ops:
  0.0 52.8 %copy-start.3 = (s32[1,8]{1,0:T(1,128)S(1)}, s32[1,8]{1,0:T(1,128)}, u32[]{:S(2)}) copy-start(s32[1,8]{1,0:T(1,128)} %lengths_ref.1) | copy-start | bytes 100
  0.0 52.8 %copy-start.2 = (s32[1,32]{1,0:T(1,128)S(1)}, s32[1,32]{1,0:T(1,128)}, u32[]{:S(2)}) copy-start(s32[1,32]{1,0:T(1,128)} %pages_ref.1) | copy-start | bytes 388
  0.0 52.8 %copy-start.1 = (bf16[1,128,2560]{2,1,0:T(8,128)(2,1)S(1)}, bf16[1,128,2560]{2,1,0:T(8,128)(2,1)}, u32[]{:S(2)}) copy-start(bf16[1,128,2560]{2,1,0:T(8,128)(2,1)} %param.7) | copy-start | bytes 1966084
  52.8 1.0 copy-start

commit v3 on v0

v3 whole, which is shorter than its diff:
```python
import math

import jax
import jax.numpy as jnp
from jax import lax
from jax.experimental import pallas as pl
from jax.experimental.pallas import tpu as pltpu
from jax.sharding import PartitionSpec as P

QUERY_HEADS = 20
KEY_VALUE_HEADS = 4
HEAD_SIZE = 128
DEVICE_TOKENS = 128
PAGE_TOKENS = 16
WIDTH = 5120
SCALE = math.log2(math.e) / math.sqrt(HEAD_SIZE)
HALF_HEADS = QUERY_HEADS // 2
HALF_WIDTH = HALF_HEADS * HEAD_SIZE
PAIR = 2 * DEVICE_TOKENS
CHUNKS = 4
CHUNK = PAIR // CHUNKS
ROWS = 2 * DEVICE_TOKENS + PAGE_TOKENS
SIZE = {"x": 4, "y": 4, "z": 8}
ORDERS = (("z", "x", "y"), ("z", "x", "y"), ("z", "y", "x"), ("z", "y", "x"), ("x", "y", "z"))
PARTS = len(ORDERS)


def place():
    g, c = lax.axis_index("group"), lax.axis_index("ctx")
    y_lo, core = lax.div(g, 2), lax.rem(g, 2)
    y_hi, z, x = lax.rem(c, 2), lax.rem(lax.div(c, 2), 8), lax.div(c, 16)
    return {"x": x, "y": y_hi * 2 + y_lo, "z": z, "core": core}


def device(at):
    return (
        lax.rem(at["y"], 2) * 2 + at["core"],
        (at["x"] * 8 + at["z"]) * 2 + lax.div(at["y"], 2),
    )


def moved(at, axis, by):
    there = dict(at)
    there[axis] = lax.rem(at[axis] + (by + SIZE[axis]), SIZE[axis])
    return there


def other_core(at):
    return {**at, "core": 1 - at["core"]}


def send(src, dst, send_sem, recv_sem, at):
    return pltpu.make_async_remote_copy(
        src_ref=src,
        dst_ref=dst,
        send_sem=send_sem,
        recv_sem=recv_sem,
        device_id=device(at),
        device_id_type=pl.DeviceIdType.MESH,
    )


def ring_block(buf, me, axis, done, position, half):
    def pick(name):
        if name == axis:
            return position
        return None if name in done else me[name]

    x, y, z = pick("x"), pick("y"), pick("z")
    everything = slice(None)
    y_lo = everything if y is None else lax.rem(y, 2)
    y_hi = everything if y is None else lax.div(y, 2)
    core = everything if half is None else half
    return buf.at[
        y_lo, core, everything if x is None else x, everything if z is None else z, y_hi
    ]


def along(me, by):
    at = lax.rem(me["x"] * 8 + me["z"] + (32 + by), 32)
    return {**me, "x": lax.div(at, 8), "z": lax.rem(at, 8)}


def slot_of(back):
    return 0 if back == 0 else 2 * back - 1 if back <= 4 else 2 * (9 - back)


def kernel(
    w_ref, hidden_ref, pages_in_ref, queries_ref, table_ref, lengths_ref, out_ref,
    ga, gb, gc, gd, ge, rem_ref, rows_ref, perm_ref, main_ref, tail_ref, wide_ref, half_ref,
    kv_ref, pool_ref, query_ref, give_ref, bias_ref, begin_ref, top_ref, total_ref, sum_ref,
    weight_send, weight_recv, mate_send, mate_recv, local_sem,
    group_send, group_recv, query_send, query_recv,
    halo_send, halo_recv, pool_send, pool_recv, give_send, give_recv,
):
    me = place()
    core = me["core"]
    mate = other_core(me)
    y_lo, y_hi = lax.rem(me["y"], 2), lax.div(me["y"], 2)
    pair = me["x"] * 8 + me["z"]
    partner = moved(me, "y", 2)
    neighbours = [mate, other_core(partner), along(me, 1), along(me, -1)] + [
        moved(me, axis, by) for axis in "xyz" for by in range(1, SIZE[axis])
    ]
    barrier = pltpu.get_barrier_semaphore()
    for at in neighbours:
        pl.semaphore_signal(
            barrier, inc=1, device_id=device(at), device_id_type=pl.DeviceIdType.MESH
        )

    own_rows = pl.ds(pl.multiple_of(core * 128, 128), 128)
    rows_stay = pltpu.make_async_copy(hidden_ref, rows_ref.at[own_rows], local_sem.at[5])
    pool_stay = pltpu.make_async_copy(pages_in_ref, rows_ref.at[pl.ds(256, 16)], local_sem.at[6])
    rows_stay.start()
    pool_stay.start()
    rest = w_ref[16:20, :].astype(jnp.float32)
    for half in range(2):
        pieces = []
        for row in range(4):
            for block in range(4):
                first = (block // 2) * 512 + half * 256 + (block % 2) * 128
                pieces.append(rest[row:row + 1, first:first + 128])
        rem_ref[half] = jnp.concatenate(pieces, axis=0).astype(jnp.bfloat16)
    row = lax.broadcasted_iota(jnp.int32, (640, 640), 0)
    col = lax.broadcasted_iota(jnp.int32, (640, 640), 1)
    last = col - 512
    source = jnp.where(
        col < 512,
        20 * lax.shift_right_logical(col, 4) + (col & 15),
        20 * lax.shift_right_logical(last, 2) + 16 + (last & 3),
    )
    perm_ref[...] = jnp.where(row == source, 1.0, 0.0).astype(jnp.bfloat16)
    pl.semaphore_wait(barrier, len(neighbours))

    bufs = (ga, gb, gc, gd, ge)

    def slot(buf, of_core):
        return buf.at[y_lo, of_core, me["x"], me["z"], y_hi]

    def shard_parts(half):
        starts = (half * 256, half * 256 + 128, half * 256 + 512, half * 256 + 640)
        return [
            w_ref.at[pl.ds(0, 16), pl.ds(pl.multiple_of(start, 128), 128)] for start in starts
        ] + [rem_ref.at[half]]

    to_mate = [
        send(src, slot(buf, core), mate_send.at[n], mate_recv.at[n], mate)
        for n, (src, buf) in enumerate(zip(shard_parts(1 - core), bufs))
    ]
    stay = [
        pltpu.make_async_copy(src, slot(buf, core), local_sem.at[n])
        for n, (src, buf) in enumerate(zip(shard_parts(core), bufs))
    ]
    for copy in to_mate + stay:
        copy.start()

    def direct(part, phase):
        order = ORDERS[part]
        axis, done = order[phase], order[:phase]
        base = 0 if phase == 0 else SIZE[order[0]] - 1
        block = ring_block(bufs[part], me, axis, done, me[axis], None)
        return [
            send(
                block, block, weight_send.at[part, base + by - 1],
                weight_recv.at[part, base + by - 1], moved(me, axis, by),
            )
            for by in range(1, SIZE[axis])
        ]

    def ring(part, step, way, half):
        order = ORDERS[part]
        axis, size = order[2], SIZE[order[2]]
        sign = 1 - 2 * way
        index = SIZE[order[0]] + SIZE[order[1]] - 2 + ((step - 1) * 2 + way) * 2 + half
        at = lax.rem(me[axis] + (size - sign * (step - 1)), size)
        block = ring_block(bufs[part], me, axis, order[:2], at, half)
        return send(
            block, block, weight_send.at[part, index], weight_recv.at[part, index],
            moved(me, axis, sign),
        )

    def ring_steps(part):
        return SIZE[ORDERS[part][2]] // 2

    def ring_sends(part):
        steps = ring_steps(part)
        return [
            (step, way, half)
            for step in range(1, steps + 1) for way in range(2) for half in range(2)
            if step < steps or half == way
        ]

    def second(part):
        for copy in direct(part, 0):
            copy.wait_recv()
        for copy in direct(part, 1):
            copy.start()

    def third(part):
        for copy in direct(part, 1):
            copy.wait_recv()
        for turn in range(2):
            for way in range(2):
                ring(part, 1, way, way ^ turn).start()

    def pass_on(part, step, turn):
        for way in range(2):
            ring(part, step, way, way ^ turn).wait_recv()
            if step + 1 < ring_steps(part) or turn == 0:
                ring(part, step + 1, way, way ^ turn).start()

    def close(part):
        steps = ring_steps(part)
        for way in range(2):
            ring(part, steps - 1, way, 1 - way).wait_recv()
        for way in range(2):
            ring(part, steps, way, way).wait_recv()

    for part in (4, 0, 2, 1, 3):
        to_mate[part].wait_recv()
        stay[part].wait()
        for copy in direct(part, 0):
            copy.start()
    rows_out = send(hidden_ref, rows_ref.at[own_rows], mate_send.at[5], mate_recv.at[5], mate)
    rows_out.start()

    def half_columns(ref, of):
        return ref.at[:, pl.ds(pl.multiple_of(of * HALF_WIDTH, 128), HALF_WIDTH)]

    query_out = send(
        half_columns(queries_ref, 1 - y_hi), query_ref.at[y_hi], query_send, query_recv, partner
    )
    query_stay = pltpu.make_async_copy(
        half_columns(queries_ref, y_hi), query_ref.at[y_hi], local_sem.at[7]
    )
    query_stay.start()

    def reorder(first, count):
        def one(number, carry):
            block = rows_ref[:, pl.ds(pl.multiple_of(number * 640, 128), 640)]
            turned = jnp.dot(block, perm_ref[...], preferred_element_type=jnp.float32)
            turned = turned.astype(jnp.bfloat16)
            main_ref[:, pl.ds(pl.multiple_of(number * 512, 128), 512)] = turned[:, :512]
            tail_ref[:, pl.ds(pl.multiple_of(number * 128, 128), 128)] = turned[:, 512:]
            return carry

        lax.fori_loop(first, first + count, one, 0)

    second(4)
    second(0)
    second(2)
    rows_stay.wait()
    pool_stay.wait()
    third(4)
    second(1)
    second(3)
    pass_on(4, 1, 0)
    pass_on(4, 1, 1)
    third(0)
    third(2)
    rows_out.wait_recv()
    reorder(0, 2)
    pass_on(4, 2, 0)
    third(1)
    third(3)
    pass_on(4, 2, 1)
    reorder(2, 2)
    pass_on(0, 1, 0)
    pass_on(2, 1, 0)
    pass_on(4, 3, 0)
    reorder(4, 2)
    pass_on(1, 1, 0)
    pass_on(3, 1, 0)
    reorder(6, 2)

    token = lax.broadcasted_iota(jnp.int32, (PAIR, PAIR), 0)
    lane = lax.broadcasted_iota(jnp.int32, (PAIR, PAIR), 1)
    position = pair * PAIR + token
    begin = jnp.zeros((PAIR, PAIR), jnp.int32)
    end = jnp.int32(0)
    for number in range(8):
        end = end + lengths_ref[0, number]
        begin = jnp.where(position >= end, end, begin)
    begin_ref[...] = begin
    top_ref[...] = jnp.full(top_ref.shape, -jnp.inf, jnp.float32)
    total_ref[...] = jnp.zeros(total_ref.shape, jnp.float32)
    sum_ref[...] = jnp.zeros(sum_ref.shape, jnp.float32)

    def bias_of(back_by):
        key = (pair - back_by) * PAIR + lane
        live = key >= begin_ref[...]
        if back_by == 0:
            live = jnp.logical_and(live, key <= position)
        return jnp.where(live, 0.0, -jnp.inf).astype(jnp.float32)

    bias_ref[:, :PAIR] = bias_of(0)

    close(4)
    wide_ref[...] = ge[...].reshape(4096, 128).astype(jnp.float32)
    rest = [
        wide_ref[pl.ds(block, 1024, stride=4), :].astype(jnp.bfloat16) for block in range(4)
    ]
    for first in (0, 2):
        both = []
        for part in (first, first + 1):
            close(part)
            both.append(bufs[part][...].reshape(4096, 128))
        total = jnp.dot(
            main_ref[...], jnp.concatenate(both, axis=1), preferred_element_type=jnp.float32
        )
        total = total + jnp.dot(
            tail_ref[...], jnp.concatenate(rest[first:first + 2], axis=1),
            preferred_element_type=jnp.float32,
        )
        half_ref[:, 128 * first:128 * first + 256] = total.astype(jnp.bfloat16)

    def regroup(number, from_hi):
        if number < 2:
            to_core = jnp.int32(number)
            src = half_ref.at[pl.ds(number * 128, 128)]
            dst = kv_ref.at[0, pl.ds(pl.multiple_of(from_hi * 128, 128), 128)]
        else:
            to_core = y_hi
            src = half_ref.at[pl.ds(256, 16)]
            dst = pool_ref.at[y_hi * 32 + pair]
        to = {**me, "y": core * 2 + y_lo, "core": to_core}
        stays = jnp.logical_and(core == y_hi, core == to_core)
        return src, dst, to, stays

    def regroup_send(number):
        src, dst, to, stays = regroup(number, y_hi)
        recv_sem = group_recv.at[y_hi] if number < 2 else group_recv.at[2]

        @pl.when(stays)
        def _():
            pltpu.make_async_copy(src, dst, recv_sem).start()

        @pl.when(jnp.logical_not(stays))
        def _():
            send(src, dst, group_send.at[number], recv_sem, to).start()

    for number in (2, 0, 1):
        regroup_send(number)
    query_out.start()

    def pool_copies(phase):
        if phase == 0:
            block, axis = pool_ref.at[pl.ds(core * 32 + pair, 1)], "z"
        else:
            block, axis = pool_ref.at[pl.ds(core * 32 + me["x"] * 8, 8)], "x"
        base = 0 if phase == 0 else SIZE["z"] - 1
        return [
            send(
                block, block, pool_send.at[base + by - 1], pool_recv.at[base + by - 1],
                moved(me, axis, by),
            )
            for by in range(1, SIZE[axis])
        ]

    half_pool = pool_ref.at[pl.ds(core * 32, 32)]
    pool_swap = send(half_pool, half_pool, pool_send.at[10], pool_recv.at[10], mate)

    def chunk(slot, number):
        return kv_ref.at[slot, pl.ds(number * CHUNK, CHUNK)]

    def forth(step, number):
        return send(
            chunk(slot_of(step - 1), number), chunk(slot_of(step), number),
            halo_send.at[step - 1, number], halo_recv.at[step - 1, number], along(me, 1),
        )

    def back(step, number):
        if step == 0:
            src, to = slot_of(0), moved(me, "x", 1)
        else:
            src, to = slot_of(9 - step), along(me, -1)
        return send(
            chunk(src, number), chunk(slot_of(8 - step), number),
            halo_send.at[4 + step, number], halo_recv.at[4 + step, number], to,
        )

    def own_arrives(from_hi):
        src = half_ref.at[pl.ds(0, 128)]
        dst = kv_ref.at[0, pl.ds(from_hi * 128, 128)]
        send(src, dst, group_send.at[0], group_recv.at[from_hi], mate).wait_recv()

    for from_hi in range(2):
        own_arrives(from_hi)
        for number in range(2 * from_hi, 2 * from_hi + 2):
            forth(1, number).start()
            back(0, number).start()
    page = pool_ref.at[core * 32 + pair]
    send(half_ref.at[pl.ds(256, 16)], page, group_send.at[2], group_recv.at[2], mate).wait_recv()
    for copy in pool_copies(0):
        copy.start()

    def attend(first, count, masked, at):
        rows = count * PAIR
        head = at // 5
        query = query_ref[:, :, at * 128:at * 128 + 128].reshape(PAIR, 128)
        key = kv_ref[first:first + count, :, head * 128:head * 128 + 128].reshape(rows, 128)
        value = kv_ref[first:first + count, :, 256 + head * 128:384 + head * 128]
        score = lax.dot_general(
            query, key, (((1,), (1,)), ((), ())), preferred_element_type=jnp.float32
        )
        if masked:
            score = score + bias_ref[:, :rows]
        old = top_ref[at]
        new = jnp.maximum(old, jnp.max(score, axis=1, keepdims=True))
        factor = jnp.exp2((old - new) * SCALE)
        weight = jnp.exp2((score - jnp.concatenate([new] * (rows // 128), axis=1)) * SCALE)
        part = weight[:, :128]
        for lanes in range(128, rows, 128):
            part = part + weight[:, lanes:lanes + 128]
        top_ref[at] = new
        total_ref[at] = total_ref[at] * factor + part
        sum_ref[at] = sum_ref[at] * factor + jnp.dot(
            weight.astype(jnp.bfloat16), value.reshape(rows, 128),
            preferred_element_type=jnp.float32,
        )

    def give(at):
        first = pl.multiple_of(y_hi * HALF_WIDTH + at * 128, 128)
        return send(
            give_ref.at[:, pl.ds(at * 128, 128)], out_ref.at[:, pl.ds(first, 128)],
            give_send.at[at], give_recv.at[at], partner,
        )

    def finish(at):
        total = jnp.sum(total_ref[at], axis=1, keepdims=True)
        done = (sum_ref[at] / total).astype(jnp.bfloat16).reshape(2, 128, 128)
        for hi in range(2):
            @pl.when(y_hi == hi)
            def _():
                first = hi * HALF_WIDTH + at * 128
                out_ref[:, first:first + 128] = done[hi]
                give_ref[:, at * 128:at * 128 + 128] = done[1 - hi]
        give(at).start()

    def stage(step):
        bias_ref[:, :PAIR] = bias_of(step)
        bias_ref[:, PAIR:] = bias_of(9 - step)

    def prompt_in():
        pool_swap.wait_recv()

        def page_in(number, carry):
            first = pl.multiple_of(lax.rem(number, 16) * 16, 16)
            at = table_ref[0, number]
            kv_ref[9 + lax.div(number, 16), pl.ds(first, 16)] = pool_ref[
                lax.rem(at, 2) * 32 + lax.div(at, 2)
            ]
            return carry

        lax.fori_loop(0, 32, page_in, 0)

    def heads(number, parts):
        return range(10 * number // parts, 10 * (number + 1) // parts)

    for step in range(1, 5):
        for number in range(CHUNKS):
            forth(step, number).wait_recv()
            if step < 4:
                forth(step + 1, number).start()
            back(step - 1, number).wait_recv()
            if step < 4:
                back(step, number).start()
            if step == 2 and number == 0:
                for copy in pool_copies(0):
                    copy.wait_recv()
                for copy in pool_copies(1):
                    copy.start()
            if step == 3 and number == 1:
                for copy in pool_copies(1):
                    copy.wait_recv()
                pool_swap.start()
            if step == 1:
                if number == CHUNKS // 2:
                    query_out.wait_recv()
                    query_stay.wait()
                if number >= CHUNKS // 2:
                    for at in heads(number - CHUNKS // 2, CHUNKS - CHUNKS // 2):
                        attend(0, 1, True, at)
            else:
                for at in heads(number, CHUNKS):
                    attend(2 * step - 3, 2, True, at)
            if step == 4:
                if number == 0:
                    prompt_in()
                for at in heads(number, CHUNKS):
                    attend(9, 2, False, at)
        stage(step)
    for at in range(10):
        attend(7, 2, True, at)
        finish(at)

    for at in range(10):
        give(at).wait()
    for copy in to_mate:
        copy.wait_send()
    rows_out.wait_send()
    query_out.wait_send()
    for part in range(PARTS):
        for phase in range(2):
            for copy in direct(part, phase):
                copy.wait_send()
        for step, way, half in ring_sends(part):
            ring(part, step, way, half).wait_send()
    for number in range(3):
        src, dst, to, stays = regroup(number, y_hi)

        @pl.when(jnp.logical_not(stays))
        def _():
            send(src, dst, group_send.at[number], group_recv.at[0], to).wait_send()

    for phase in range(2):
        for copy in pool_copies(phase):
            copy.wait_send()
    pool_swap.wait_send()
    for step in range(1, 5):
        for number in range(CHUNKS):
            forth(step, number).wait_send()
            back(step - 1, number).wait_send()


def body(hidden, queries, key_value_weight, pooled_hidden_states, group_page_table, resp_lengths):
    in_hbm = pl.BlockSpec(memory_space=pl.ANY)
    in_vmem = pl.BlockSpec(memory_space=pltpu.VMEM)
    in_smem = pl.BlockSpec(memory_space=pltpu.SMEM)
    dma = pltpu.SemaphoreType.DMA
    shards = pltpu.VMEM((2, 2, 4, 8, 2, 16, 128), jnp.bfloat16)
    sums = pltpu.VMEM((HALF_HEADS, PAIR, 128), jnp.float32)
    out = pl.pallas_call(
        kernel,
        name="attend",
        out_shape=jax.ShapeDtypeStruct((DEVICE_TOKENS, QUERY_HEADS * HEAD_SIZE), jnp.bfloat16),
        in_specs=[in_vmem, in_hbm, in_hbm, in_hbm, in_smem, in_smem],
        out_specs=in_vmem,
        scratch_shapes=[
            shards, shards, shards, shards, shards,
            pltpu.VMEM((2, 16, 128), jnp.bfloat16),
            pltpu.VMEM((ROWS, WIDTH), jnp.bfloat16),
            pltpu.VMEM((640, 640), jnp.bfloat16),
            pltpu.VMEM((ROWS, 4096), jnp.bfloat16),
            pltpu.VMEM((ROWS, 1024), jnp.bfloat16),
            pltpu.VMEM((4096, 128), jnp.float32),
            pltpu.VMEM((ROWS, 512), jnp.bfloat16),
            pltpu.VMEM((11, PAIR, 512), jnp.bfloat16),
            pltpu.VMEM((64, PAGE_TOKENS, 512), jnp.bfloat16),
            pltpu.VMEM((2, DEVICE_TOKENS, HALF_WIDTH), jnp.bfloat16),
            pltpu.VMEM((DEVICE_TOKENS, HALF_WIDTH), jnp.bfloat16),
            pltpu.VMEM((PAIR, 2 * PAIR), jnp.float32),
            pltpu.VMEM((PAIR, PAIR), jnp.int32),
            sums, sums, sums,
            dma((PARTS, 26)), dma((PARTS, 26)), dma((6,)), dma((6,)), dma((8,)),
            dma((3,)), dma((3,)), dma, dma,
            dma((8, CHUNKS)), dma((8, CHUNKS)), dma((11,)), dma((11,)),
            dma((HALF_HEADS,)), dma((HALF_HEADS,)),
        ],
        compiler_params=pltpu.CompilerParams(
            collective_id=0, has_side_effects=True, vmem_limit_bytes=56 * 1024 * 1024
        ),
    )(
        key_value_weight, hidden[0], pooled_hidden_states[0], queries[0],
        group_page_table, resp_lengths,
    )
    return out[None]


def solution(mesh):
    in_specs = (
        P("group", "ctx", None),
        P("group", "ctx", None),
        P(("group", "ctx"), None),
        P("ctx", None, None),
        P("group", None),
        P("group", None),
    )
    out_specs = P("group", "ctx", None)
    return jax.shard_map(body, mesh=mesh, in_specs=in_specs, out_specs=out_specs, check_vma=False)
```

time: 1160 us -> 112 us (0.10)
  the two profiles are of different devices: /device:TPU:14 before, /device:TPU:9 now
where the time goes in v3:
time: 112 us
  Pallas kernels  110 us (98%)
  local copies, waits for them, and re-layouts  1.97 us (2%)
    pallas_call x1, Pallas kernels, body(): pl.pallas_call(kernel, name='attend', out_shape=jax.ShapeDtypeStruct((DEV...  110 us

profile of v3, /device:TPU:9, one launch (start us, length us, event | category | flops | bytes accessed | tf_op | source)
XLA Modules:
  0.0 111.6 jit_solution(5217490602596500727)
XLA Ops:
  0.0 109.7 %attend.1 = bf16[128,2560]{1,0:T(8,128)(2,1)} custom-call(bf16[20,1024]{1,0:T(8,128)(2,1)} %w_ref.1, bf16[128,5120]{1,0:T(8,128)(2,1)} %bitcast.5, bf16[16,5120]{1,0:T(8,128)(2,1)} %bitcast.7, bf16[128,2560]{1,0:T(8,128)(2,1)} %bitcast.6, s32[1,32]{1,0:T(1,128)} %table_ref.1, s32[1,8]{1,0:T(1,128)} %lengths_ref.1), custom_call_target="tpu_custom_call" | custom-call | tf_op jit(solution)/shard_map/attend/pallas_call | solution.py:533
  109.7 2.0 %copy.8 = bf16[1,128,2560]{2,1,0:T(8,128)(2,1)} copy(bf16[1,128,2560]{2,1,0:T(8,128)(2,1)} %bitcast.4) | data formatting | bytes 1310720

commit v4 on v3

--- a/solution.py
+++ b/solution.py
@@ -17,8 +17,9 @@
 HALF_HEADS = QUERY_HEADS // 2
 HALF_WIDTH = HALF_HEADS * HEAD_SIZE
 PAIR = 2 * DEVICE_TOKENS
-CHUNKS = 4
-CHUNK = PAIR // CHUNKS
+ROW_CHUNKS = 2
+CHUNKS = 2 * ROW_CHUNKS
+CHUNK = PAIR // ROW_CHUNKS
 ROWS = 2 * DEVICE_TOKENS + PAGE_TOKENS
 SIZE = {"x": 4, "y": 4, "z": 8}
 ORDERS = (("z", "x", "y"), ("z", "x", "y"), ("z", "y", "x"), ("z", "y", "x"), ("x", "y", "z"))
@@ -312,24 +313,27 @@
             tail_ref[...], jnp.concatenate(rest[first:first + 2], axis=1),
             preferred_element_type=jnp.float32,
         )
-        half_ref[:, 128 * first:128 * first + 256] = total.astype(jnp.bfloat16)
+        total = total.astype(jnp.bfloat16)
+        for head in range(2):
+            half_ref[head, :, 64 * first:64 * first + 128] = total[:, 128 * head:128 * head + 128]
 
     def regroup(number, from_hi):
-        if number < 2:
-            to_core = jnp.int32(number)
-            src = half_ref.at[pl.ds(number * 128, 128)]
-            dst = kv_ref.at[0, pl.ds(pl.multiple_of(from_hi * 128, 128), 128)]
+        if number < 4:
+            head, to_core = number // 2, jnp.int32(number % 2)
+            src = half_ref.at[head, pl.ds((number % 2) * 128, 128)]
+            dst = kv_ref.at[head, 0, pl.ds(pl.multiple_of(from_hi * 128, 128), 128)]
+            recv_sem = group_recv.at[head, from_hi]
         else:
             to_core = y_hi
-            src = half_ref.at[pl.ds(256, 16)]
-            dst = pool_ref.at[y_hi * 32 + pair]
+            src = half_ref.at[y_lo, pl.ds(256, 16)]
+            dst = pool_ref.at[y_hi * 32 + pair, y_lo]
+            recv_sem = group_recv.at[2, 0]
         to = {**me, "y": core * 2 + y_lo, "core": to_core}
         stays = jnp.logical_and(core == y_hi, core == to_core)
-        return src, dst, to, stays
+        return src, dst, recv_sem, to, stays
 
     def regroup_send(number):
-        src, dst, to, stays = regroup(number, y_hi)
-        recv_sem = group_recv.at[y_hi] if number < 2 else group_recv.at[2]
+        src, dst, recv_sem, to, stays = regroup(number, y_hi)
 
         @pl.when(stays)
         def _():
@@ -339,15 +343,15 @@
         def _():
             send(src, dst, group_send.at[number], recv_sem, to).start()
 
-    for number in (2, 0, 1):
+    for number in range(5):
         regroup_send(number)
     query_out.start()
 
     def pool_copies(phase):
         if phase == 0:
-            block, axis = pool_ref.at[pl.ds(core * 32 + pair, 1)], "z"
+            block, axis = pool_ref.at[pl.ds(core * 32 + pair, 1), y_lo], "z"
         else:
-            block, axis = pool_ref.at[pl.ds(core * 32 + me["x"] * 8, 8)], "x"
+            block, axis = pool_ref.at[pl.ds(core * 32 + me["x"] * 8, 8), y_lo], "x"
         base = 0 if phase == 0 else SIZE["z"] - 1
         return [
             send(
@@ -357,11 +361,17 @@
             for by in range(1, SIZE[axis])
         ]
 
+    one_head = pool_ref.at[pl.ds(core * 32, 32), y_lo]
+    pool_heads = send(
+        one_head, one_head, pool_send.at[10], pool_recv.at[10],
+        {**me, "y": y_hi * 2 + 1 - y_lo},
+    )
     half_pool = pool_ref.at[pl.ds(core * 32, 32)]
-    pool_swap = send(half_pool, half_pool, pool_send.at[10], pool_recv.at[10], mate)
+    pool_swap = send(half_pool, half_pool, pool_send.at[11], pool_recv.at[11], mate)
 
     def chunk(slot, number):
-        return kv_ref.at[slot, pl.ds(number * CHUNK, CHUNK)]
+        head, part = number % 2, number // 2
+        return kv_ref.at[head, slot, pl.ds(part * CHUNK, CHUNK)]
 
     def forth(step, number):
         return send(
@@ -379,18 +389,16 @@
             halo_send.at[4 + step, number], halo_recv.at[4 + step, number], to,
         )
 
-    def own_arrives(from_hi):
-        src = half_ref.at[pl.ds(0, 128)]
-        dst = kv_ref.at[0, pl.ds(from_hi * 128, 128)]
-        send(src, dst, group_send.at[0], group_recv.at[from_hi], mate).wait_recv()
-
-    for from_hi in range(2):
-        own_arrives(from_hi)
-        for number in range(2 * from_hi, 2 * from_hi + 2):
-            forth(1, number).start()
-            back(0, number).start()
-    page = pool_ref.at[core * 32 + pair]
-    send(half_ref.at[pl.ds(256, 16)], page, group_send.at[2], group_recv.at[2], mate).wait_recv()
+    for number in range(CHUNKS):
+        head, from_hi = number % 2, number // 2
+        src = half_ref.at[head, pl.ds(0, 128)]
+        dst = kv_ref.at[head, 0, pl.ds(from_hi * 128, 128)]
+        send(src, dst, group_send.at[head], group_recv.at[head, from_hi], mate).wait_recv()
+        forth(1, number).start()
+        back(0, number).start()
+    page = pool_ref.at[core * 32 + pair, y_lo]
+    page_here = half_ref.at[y_lo, pl.ds(256, 16)]
+    send(page_here, page, group_send.at[4], group_recv.at[2, 0], mate).wait_recv()
     for copy in pool_copies(0):
         copy.start()
 
@@ -398,8 +406,8 @@
         rows = count * PAIR
         head = at // 5
         query = query_ref[:, :, at * 128:at * 128 + 128].reshape(PAIR, 128)
-        key = kv_ref[first:first + count, :, head * 128:head * 128 + 128].reshape(rows, 128)
-        value = kv_ref[first:first + count, :, 256 + head * 128:384 + head * 128]
+        key = kv_ref[head, first:first + count, :, :128].reshape(rows, 128)
+        value = kv_ref[head, first:first + count, :, 128:]
         score = lax.dot_general(
             query, key, (((1,), (1,)), ((), ())), preferred_element_type=jnp.float32
         )
@@ -447,9 +455,9 @@
         def page_in(number, carry):
             first = pl.multiple_of(lax.rem(number, 16) * 16, 16)
             at = table_ref[0, number]
-            kv_ref[9 + lax.div(number, 16), pl.ds(first, 16)] = pool_ref[
-                lax.rem(at, 2) * 32 + lax.div(at, 2)
-            ]
+            rows = pool_ref[lax.rem(at, 2) * 32 + lax.div(at, 2)]
+            for head in range(2):
+                kv_ref[head, 9 + lax.div(number, 16), pl.ds(first, 16)] = rows[head]
             return carry
 
         lax.fori_loop(0, 32, page_in, 0)
@@ -457,42 +465,47 @@
     def heads(number, parts):
         return range(10 * number // parts, 10 * (number + 1) // parts)
 
-    for step in range(1, 5):
+    for step in range(1, 4):
         for number in range(CHUNKS):
+            back(step - 1, number).wait_recv()
+            back(step, number).start()
             forth(step, number).wait_recv()
-            if step < 4:
-                forth(step + 1, number).start()
-            back(step - 1, number).wait_recv()
-            if step < 4:
-                back(step, number).start()
+            forth(step + 1, number).start()
             if step == 2 and number == 0:
                 for copy in pool_copies(0):
                     copy.wait_recv()
                 for copy in pool_copies(1):
                     copy.start()
-            if step == 3 and number == 1:
+            if step == 1 and number == 2:
+                query_out.wait_recv()
+                query_stay.wait()
+            if step == 3 and number == 0:
                 for copy in pool_copies(1):
                     copy.wait_recv()
+                pool_heads.start()
+            if step == 3 and number == 3:
+                pool_heads.wait_recv()
                 pool_swap.start()
-            if step == 1:
-                if number == CHUNKS // 2:
-                    query_out.wait_recv()
-                    query_stay.wait()
-                if number >= CHUNKS // 2:
-                    for at in heads(number - CHUNKS // 2, CHUNKS - CHUNKS // 2):
-                        attend(0, 1, True, at)
-            else:
+            if step > 1:
                 for at in heads(number, CHUNKS):
                     attend(2 * step - 3, 2, True, at)
-            if step == 4:
-                if number == 0:
-                    prompt_in()
-                for at in heads(number, CHUNKS):
-                    attend(9, 2, False, at)
+            elif number >= CHUNKS // 2:
+                for at in heads(number - CHUNKS // 2, CHUNKS - CHUNKS // 2):
+                    attend(0, 1, True, at)
         stage(step)
     for at in range(10):
-        attend(7, 2, True, at)
-        finish(at)
+        attend(5, 2, True, at)
+    stage(4)
+    prompt_in()
+    for head in range(2):
+        for at in range(5 * head, 5 * head + 5):
+            attend(9, 2, False, at)
+        for number in range(head, CHUNKS, 2):
+            forth(4, number).wait_recv()
+            back(3, number).wait_recv()
+        for at in range(5 * head, 5 * head + 5):
+            attend(7, 2, True, at)
+            finish(at)
 
     for at in range(10):
         give(at).wait()
@@ -506,16 +519,17 @@
                 copy.wait_send()
         for step, way, half in ring_sends(part):
             ring(part, step, way, half).wait_send()
-    for number in range(3):
-        src, dst, to, stays = regroup(number, y_hi)
+    for number in range(5):
+        src, dst, recv_sem, to, stays = regroup(number, y_hi)
 
         @pl.when(jnp.logical_not(stays))
         def _():
-            send(src, dst, group_send.at[number], group_recv.at[0], to).wait_send()
+            send(src, dst, group_send.at[number], recv_sem, to).wait_send()
 
     for phase in range(2):
         for copy in pool_copies(phase):
             copy.wait_send()
+    pool_heads.wait_send()
     pool_swap.wait_send()
     for step in range(1, 5):
         for number in range(CHUNKS):
@@ -544,17 +558,17 @@
             pltpu.VMEM((ROWS, 4096), jnp.bfloat16),
             pltpu.VMEM((ROWS, 1024), jnp.bfloat16),
             pltpu.VMEM((4096, 128), jnp.float32),
-            pltpu.VMEM((ROWS, 512), jnp.bfloat16),
-            pltpu.VMEM((11, PAIR, 512), jnp.bfloat16),
-            pltpu.VMEM((64, PAGE_TOKENS, 512), jnp.bfloat16),
+            pltpu.VMEM((2, ROWS, 256), jnp.bfloat16),
+            pltpu.VMEM((2, 11, PAIR, 256), jnp.bfloat16),
+            pltpu.VMEM((64, 2, PAGE_TOKENS, 256), jnp.bfloat16),
             pltpu.VMEM((2, DEVICE_TOKENS, HALF_WIDTH), jnp.bfloat16),
             pltpu.VMEM((DEVICE_TOKENS, HALF_WIDTH), jnp.bfloat16),
             pltpu.VMEM((PAIR, 2 * PAIR), jnp.float32),
             pltpu.VMEM((PAIR, PAIR), jnp.int32),
             sums, sums, sums,
             dma((PARTS, 26)), dma((PARTS, 26)), dma((6,)), dma((6,)), dma((8,)),
-            dma((3,)), dma((3,)), dma, dma,
-            dma((8, CHUNKS)), dma((8, CHUNKS)), dma((11,)), dma((11,)),
+            dma((5,)), dma((3, 2)), dma, dma,
+            dma((8, CHUNKS)), dma((8, CHUNKS)), dma((12,)), dma((12,)),
             dma((HALF_HEADS,)), dma((HALF_HEADS,)),
         ],
         compiler_params=pltpu.CompilerParams(

time: 112 us -> 114 us (1.018)
  the two profiles are of different devices: /device:TPU:9 before, /device:TPU:4 now
where the time goes in v4:
time: 114 us
  Pallas kernels  112 us (98%)
  local copies, waits for them, and re-layouts  1.97 us (2%)
    pallas_call x1, Pallas kernels, body(): pl.pallas_call(kernel, name='attend', out_shape=jax.ShapeDtypeStruct((DEV...  112 us

profile of v4, /device:TPU:4, one launch (start us, length us, event | category | flops | bytes accessed | tf_op | source)
XLA Modules:
  0.0 113.9 jit_solution(8448083508222709189)
XLA Ops:
  0.0 111.9 %attend.1 = bf16[128,2560]{1,0:T(8,128)(2,1)} custom-call(bf16[20,1024]{1,0:T(8,128)(2,1)} %w_ref.1, bf16[128,5120]{1,0:T(8,128)(2,1)} %bitcast.5, bf16[16,5120]{1,0:T(8,128)(2,1)} %bitcast.7, bf16[128,2560]{1,0:T(8,128)(2,1)} %bitcast.6, s32[1,32]{1,0:T(1,128)} %table_ref.1, s32[1,8]{1,0:T(1,128)} %lengths_ref.1), custom_call_target="tpu_custom_call" | custom-call | tf_op jit(solution)/shard_map/attend/pallas_call | solution.py:547
  111.9 2.0 %copy.8 = bf16[1,128,2560]{2,1,0:T(8,128)(2,1)} copy(bf16[1,128,2560]{2,1,0:T(8,128)(2,1)} %bitcast.4) | data formatting | bytes 1310720

commit v5 on v3

--- a/solution.py
+++ b/solution.py
@@ -457,14 +457,12 @@
     def heads(number, parts):
         return range(10 * number // parts, 10 * (number + 1) // parts)
 
-    for step in range(1, 5):
+    for step in range(1, 4):
         for number in range(CHUNKS):
             forth(step, number).wait_recv()
-            if step < 4:
-                forth(step + 1, number).start()
+            forth(step + 1, number).start()
             back(step - 1, number).wait_recv()
-            if step < 4:
-                back(step, number).start()
+            back(step, number).start()
             if step == 2 and number == 0:
                 for copy in pool_copies(0):
                     copy.wait_recv()
@@ -484,12 +482,16 @@
             else:
                 for at in heads(number, CHUNKS):
                     attend(2 * step - 3, 2, True, at)
-            if step == 4:
-                if number == 0:
-                    prompt_in()
-                for at in heads(number, CHUNKS):
-                    attend(9, 2, False, at)
         stage(step)
+    for at in range(10):
+        attend(5, 2, True, at)
+    prompt_in()
+    for at in range(10):
+        attend(9, 2, False, at)
+    stage(4)
+    for number in range(CHUNKS):
+        forth(4, number).wait_recv()
+        back(3, number).wait_recv()
     for at in range(10):
         attend(7, 2, True, at)
         finish(at)

time: 112 us -> 111 us (level)
  no operation moved by 1% of the time
where the time goes in v5:
time: 111 us
  Pallas kernels  109 us (98%)
  local copies, waits for them, and re-layouts  1.97 us (2%)
    pallas_call x1, Pallas kernels, body(): pl.pallas_call(kernel, name='attend', out_shape=jax.ShapeDtypeStruct((DEV...  109 us

profile of v5, /device:TPU:9, one launch (start us, length us, event | category | flops | bytes accessed | tf_op | source)
XLA Modules:
  0.0 111.1 jit_solution(2214290545187392379)
XLA Ops:
  0.0 109.2 %attend.1 = bf16[128,2560]{1,0:T(8,128)(2,1)} custom-call(bf16[20,1024]{1,0:T(8,128)(2,1)} %w_ref.1, bf16[128,5120]{1,0:T(8,128)(2,1)} %bitcast.5, bf16[16,5120]{1,0:T(8,128)(2,1)} %bitcast.7, bf16[128,2560]{1,0:T(8,128)(2,1)} %bitcast.6, s32[1,32]{1,0:T(1,128)} %table_ref.1, s32[1,8]{1,0:T(1,128)} %lengths_ref.1), custom_call_target="tpu_custom_call" | custom-call | tf_op jit(solution)/shard_map/attend/pallas_call | solution.py:535
  109.2 2.0 %copy.8 = bf16[1,128,2560]{2,1,0:T(8,128)(2,1)} copy(bf16[1,128,2560]{2,1,0:T(8,128)(2,1)} %bitcast.4) | data formatting | bytes 1310720
